TPU v7x, 32 devices: a whole 2x2x4 slice. The times are simulated.
32 devices in a mesh: lon: 4 (over y, x), lat: 8 (over z, core).
Axes of the slice: x: 2, y: 2, z: 4, core: 2. Of those that a mesh axis runs over, the one named last changes fastest.
Arguments:
- fields: float32 [8, 8, 240, 2880], P(None, None, 'lat', 'lon'), may hold values from -6 to 6
- mask: int32 [240], P('lat'), may hold values from 0 to 1, as said below
- cutoff: int32 [240], P('lat'), may hold values from 1 to 128, as said below
Outputs:
- updated: float32 [8, 8, 240, 2880], P(None, None, 'lat', 'lon')
Inputs may be any that keep to these rules, and one draw needn't show every extreme that they name: `mask`: nonzero only within 40 rows of either pole; row 0 is always 1. `cutoff`: both ends are taken in every draw.
All inputs are finite; a program needn't handle non-finite values.
Results may differ from a plain program's by a relative error of at most 0.00005.
Values sent between devices are 32-bit elements; how exact they have to be, the bound alone decides.
A program may use at most 64 MiB of HBM per device.

v0:
```python
import math

import jax
import jax.numpy as jnp
from jax import lax
from jax.sharding import PartitionSpec as P

KMAX = 128


def passed_along(block, axis, distance):
    devices = range(lax.axis_size(axis))
    route = [((i - distance) % len(devices), i) for i in devices]
    return lax.ppermute(block, axis, route)


def with_halo(block, sides, width, periodic):
    for axis, dim in sides:
        count = lax.axis_size(axis)
        forward = [(i, i + 1) for i in range(count - 1)]
        if periodic:
            forward.append((count - 1, 0))
        backward = [(target, source) for source, target in forward]
        low = lax.ppermute(
            lax.slice_in_dim(block, block.shape[dim] - width, None, axis=dim), axis, forward
        )
        high = lax.ppermute(lax.slice_in_dim(block, 0, width, axis=dim), axis, backward)
        block = jnp.concatenate([low, block, high], axis=dim)
    return block


def tendencies(north, south, east, west, cos_north, cos_south, dlon, dlat):
    press_t = -(
        (east[1] - west[1]) / (2.0 * dlon)
        + (cos_north * north[2] - cos_south * south[2]) / (2.0 * dlat)
    )
    zonal_t = -(east[0] - west[0]) / (2.0 * dlon)
    merid_t = -(north[0] - south[0]) / (2.0 * dlat)
    scalar_t = -(
        (east[1] * east[3:] - west[1] * west[3:]) / (2.0 * dlon)
        + (cos_north * north[2] * north[3:] - cos_south * south[2] * south[3:]) / (2.0 * dlat)
    )
    return jnp.concatenate([press_t[None], zonal_t[None], merid_t[None], scalar_t], axis=0)


def fourier_table(columns, nlon, kept):
    wavenum = jnp.arange(kept, dtype=jnp.int32)
    phase = (columns[:, None] * wavenum[None, :] % nlon).astype(jnp.float32) * (
        2.0 * math.pi / nlon
    )
    return jnp.concatenate([jnp.cos(phase), jnp.sin(phase)], axis=1)


def shards(fields, mask, cutoff):
    nfields, nlev, lat_dev, lon_dev = fields.shape
    lon_count = lax.axis_size("lon")
    lat_count = lax.axis_size("lat")
    nlon = lon_dev * lon_count
    nlat = lat_dev * lat_count
    dlon = 2.0 * math.pi / nlon
    dlat = math.pi / nlat
    step = 0.4 * dlon
    lat_pos = lax.axis_index("lat")
    lon_pos = lax.axis_index("lon")
    index = jnp.arange(nfields)
    signs = jnp.where((index == 1) | (index == 2), -1.0, 1.0).astype(jnp.float32)[:, None, None]
    pole_row = jnp.where(lat_pos == 0, fields[:, :, 0, :], fields[:, :, -1, :])
    across = passed_along(pole_row, "lon", lon_count // 2) * signs
    banded = with_halo(fields, (("lat", 2),), 1, False)
    low = jnp.where(lat_pos == 0, across, banded[:, :, 0, :])
    high = jnp.where(lat_pos == lat_count - 1, across, banded[:, :, -1, :])
    padded = jnp.concatenate([low[:, :, None], fields, high[:, :, None]], axis=2)
    wide = with_halo(fields, (("lon", 3),), 1, True)
    rows = jnp.clip(lat_pos * lat_dev + jnp.arange(lat_dev + 2) - 1, 0, nlat - 1)
    cosine = jnp.cos(-math.pi / 2 + (rows.astype(jnp.float32) + 0.5) * dlat)
    tend = tendencies(
        padded[:, :, 2:],
        padded[:, :, :-2],
        wide[..., 2:],
        wide[..., :-2],
        cosine[2:][:, None],
        cosine[:-2][:, None],
        dlon,
        dlat,
    )
    kept = KMAX
    wavenum = jnp.arange(kept)
    scale = jnp.where(wavenum == 0, 1.0 / nlon, 2.0 / nlon).astype(jnp.float32)
    keep = (wavenum[None, :] < cutoff[:, None]).astype(jnp.float32) * scale[None, :]
    weights = jnp.concatenate([keep, keep], axis=1)
    flat = tend.reshape(nfields * nlev, lat_dev, lon_dev)
    local_cols = lon_pos * lon_dev + jnp.arange(lon_dev, dtype=jnp.int32)
    table = fourier_table(local_cols, nlon, kept)
    spec = jnp.einsum("frc,ck->frk", flat, table, precision=lax.Precision.HIGHEST)
    spec = lax.psum(spec, "lon")
    proj = jnp.einsum("frk,ck->frc", spec * weights[None], table, precision=lax.Precision.HIGHEST)
    proj = proj.reshape(nfields, nlev, lat_dev, lon_dev)
    maskf = mask.astype(jnp.float32)[None, None, :, None]
    filtered = tend + maskf * (proj - tend)
    return fields + step * filtered


def solution(mesh):
    placed = (P(None, None, "lat", "lon"), P("lat"), P("lat"))
    return jax.shard_map(
        shards, mesh=mesh, in_specs=placed, out_specs=P(None, None, "lat", "lon"), check_vma=False
    )
```

profile of v0, /device:TPU:0, one launch (start us, length us, event | category | flops | bytes accessed | tf_op | source)
XLA Modules:
  0.0 134.5 jit_solution(118643007347864194)
XLA Ops:
  6.5 1.8 %fusion.35 = (f32[8,8,1,720]{3,1,0,2:T(8,128)}, f32[8,8,1,720]{3,1,0,2:T(8,128)}, f32[8,8,720]{2,1,0:T(8,128)}) fusion(pred[]{:T(512)S(6)} %eq.34, f32[8,8,30,720]{3,1,2,0:T(8,128)} %param.3), kind=kLoop, calls=%fused_computation.60 | loop fusion | flops 46080 | bytes 946177 | tf_op jit(solution)/shard_map/slice | solution.py:67
  8.4 1.3 collective-permute-start.3
  9.7 3.7 %collective-permute-start.4 = (f32[8,8,1,720]{3,1,0,2:T(8,128)}, f32[8,8,1,720]{3,1,0,2:T(8,128)}, u32[]{:S(2)}, u32[]{:S(2)}) collective-permute-start(f32[8,8,1,720]{3,1,0,2:T(8,128)} %get-tuple-element.15), channel_id=1, source_target_pairs={{0,1},{1,2},{2,3},{3,4},{4,5},{5,6},{6,7},{8,9},{9,10},{10,11},{11... | collective-permute-start | bytes 552968 | tf_op jit(solution)/shard_map/ppermute | solution.py:24
  13.4 3.0 %collective-permute-start.2 = (f32[8,8,720]{2,1,0:T(8,128)}, f32[8,8,720]{2,1,0:T(8,128)}, u32[]{:S(2)}, u32[]{:S(2)}) collective-permute-start(f32[8,8,720]{2,1,0:T(8,128)} %get-tuple-element.16), channel_id=1, source_target_pairs={{16,0},{24,8},{0,16},{8,24},{17,1},{25,9},{1,17},{9,25},{18,2},{26... | collective-permute-start | bytes 552968 | tf_op jit(solution)/shard_map/ppermute | solution.py:14
  16.3 1.8 %fusion.34 = (f32[8,8,30,1]{3,1,2,0:T(8,128)S(1)}, f32[8,8,30,1]{3,1,2,0:T(8,128)S(1)}) fusion(f32[8,8,30,720]{3,1,2,0:T(8,128)} %param.3), kind=kLoop, calls=%fused_computation.59 | loop fusion | bytes 30720 | tf_op jit(solution)/shard_map/slice | solution.py:27
  18.2 0.5 copy.31
  18.7 1.5 %collective-permute-start.1 = (f32[8,8,30,1]{2,1,3,0:T(8,128)S(1)}, f32[8,8,30,1]{2,1,3,0:T(8,128)S(1)}, u32[]{:S(2)}, u32[]{:S(2)}) collective-permute-start(f32[8,8,30,1]{2,1,3,0:T(8,128)S(1)} %copy.31), channel_id=1, source_target_pairs={{0,8},{8,16},{16,24},{24,0},{1,9},{9,17},{17,25},{25,1},{2,10},{10... | collective-permute-start | bytes 23048 | tf_op jit(solution)/shard_map/ppermute | solution.py:24
  20.2 0.5 copy.30
  20.7 1.5 %collective-permute-start = (f32[8,8,30,1]{2,1,3,0:T(8,128)S(1)}, f32[8,8,30,1]{2,1,3,0:T(8,128)S(1)}, u32[]{:S(2)}, u32[]{:S(2)}) collective-permute-start(f32[8,8,30,1]{2,1,3,0:T(8,128)S(1)} %copy.30), channel_id=1, source_target_pairs={{8,0},{16,8},{24,16},{0,24},{9,1},{17,9},{25,17},{1,25},{10,2},{18... | collective-permute-start | bytes 23048 | tf_op jit(solution)/shard_map/ppermute | solution.py:27
  22.2 2.6 %fusion.27 = (f32[720,128]{1,0:T(8,128)}, f32[720,128]{1,0:T(8,128)}) fusion(s32[720]{0:T(1024)S(1)} %iota_add_fusion), kind=kLoop, calls=%fused_computation.43 | loop fusion | flops 829440 | bytes 740160 | tf_op jit(solution)/shard_map/cos | solution.py:51
  24.8 0.1 fusion.36
  24.9 1.0 copy.20
  25.9 1.0 copy.22
  26.9 1.4 %fusion.30 = (f32[8,8,1,720]{3,1,0,2:T(8,128)S(1)}, f32[8,8,1,720]{3,1,0,2:T(8,128)S(1)}) fusion(f32[8,8,1,720]{3,1,0,2:T(8,128)} %collective-permute-done.3, f32[8,8,720]{2,1,0:T(8,128)} %collective-permute-done.2, f32[8]{0:T(128)S(1)} %or_select_fusion, pred[]{:T(512)S(6)} %eq.33, f32[8,8,1,720]{3,1,0,2:T(8,128)} %collective-permute-done.4, pred[]{:T(512)S(6)} %eq.34), kind=kLoop, calls=%fused_computation.48 | loop fusion | flops 138240 | bytes 921634 | tf_op jit(solution)/shard_map/broadcast_in_dim | solution.py:72
  28.3 0.0 slice-start.1
  28.3 3.9 %add_negate_fusion = (f32[1,8,30,720]{3,1,0,2:T(8,128)S(1)}, f32[1,8,30,720]{3,1,0,2:T(8,128)S(1)}, f32[1,8,30,720]{3,1,0,2:T(8,128)S(1)}, f32[1,8,30,720]{3,1,0...) fusion(f32[8,8,30,1]{3,1,0,2:T(8,128)S(1)} %copy.20, ...), kind=kLoop, calls=%fused_computation.35 | loop fusion | flops 3801600 | bytes 10752240 | tf_op jit(solution)/shard_map/neg | solution.py:33
  32.3 3.5 %fusion.10 = f32[5,8,30,720]{3,1,0,2:T(8,128)S(1)} fusion(f32[8,8,1,720]{3,1,0,2:T(8,128)S(1)} %get-tuple-element.18, f32[8,8,1,720]{3,1,0,2:T(8,128)S(1)} %get-tuple-element.17, f32[8,8,30,1]{3,1,0,2:T(8,128)S(1)} %copy.22, f32[8,8,30,1]{3,1,0,2:T(8,128)S(1)} %copy.20, f32[8,30,720]{2,0,1:T(8,128)S(1)} %bitcast.40, f32[8,30,720]{2,0,1:T(8,128)S(1)} %bitcast.39, ...), kind=kLoop, calls=%fused_computation.13 | loop fusion | flops 12096000 | bytes 12134400 | tf_op jit(solution)/shard_map/neg | solution.py:39
  35.8 1.8 %copy-done = f32[5,8,30,720]{3,1,0,2:T(8,128)} copy-done((f32[5,8,30,720]{3,1,0,2:T(8,128)}, f32[5,8,30,720]{3,1,0,2:T(8,128)S(1)}, u32[]{:S(2)}) %copy-start) | copy-done | bytes 3456024
  37.6 6.3 %fusion.4 = f32[64,30,256]{2,0,1:T(8,128)} fusion(f32[5,8,30,720]{3,1,0,2:T(8,128)S(1)} %fusion.10, f32[1,8,30,720]{3,1,0,2:T(8,128)S(1)} %get-tuple-element.11, f32[1,8,30,720]{3,1,0,2:T(8,128)S(1)} %get-tuple-element.10, f32[1,8,30,720]{3,1,0,2:T(8,128)S(1)} %get-tuple-element.5, f32[720,128]{1,0:T(8,128)S(1)} %copy-done.4, f32[720,128]{1,0:T(8,128)S(1)} %copy-done.2), kind=kOutput, calls=%fused_computation.6 | convolution fusion | flops 4251064320 | bytes 8232960 | tf_op jit(solution)/shard_map/frc,ck->frk/dot_general | solution.py:94
  44.0 0.0 all-reduce.2.cloned.1.call-update
  44.1 0.1 fusion.31
  44.1 68.4 %all-reduce.2.cloned.1.call-done = f32[64,30,256]{2,0,1:T(8,128)} async-done(((f32[64,30,256]{2,0,1:T(8,128)}), f32[64,30,256]{2,0,1:T(8,128)}) %all-reduce.2.cloned.1.call-update) | async-done | bytes 1966096 | tf_op jit(solution)/shard_map/psum | solution.py:95
  112.5 11.9 %fusion.3 = f32[8,8,30,720]{3,1,0,2:T(8,128)S(1)} fusion(f32[5,8,30,720]{3,1,0,2:T(8,128)} %copy-done, f32[1,8,30,720]{3,1,0,2:T(8,128)} %copy-done.1, f32[1,8,30,720]{3,1,0,2:T(8,128)S(1)} %get-tuple-element.10, f32[1,8,30,720]{3,1,0,2:T(8,128)S(1)} %get-tuple-element.5, f32[30]{0:T(128)S(1)} %convert_element_type.11, ...), kind=kOutput, calls=%fused_computation.5 | convolution fusion | flops 4258467840 | bytes 19323000 | tf_op jit(solution)/shard_map/frk,ck->frc/dot_general | solution.py:96
  124.5 3.2 %copy.29 = f32[8,8,30,720]{3,1,2,0:T(8,128)} copy(f32[8,8,30,720]{3,1,0,2:T(8,128)S(1)} %fusion.3) | data formatting | bytes 11059200 | tf_op jit(solution)/shard_map/add | solution.py:100
  (31 shorter events, 0.1 us)
Async XLA Ops:
  6.5 106.0 %all-reduce.2.cloned.1.call-start = ((), (), s32[]{:S(2)}) async-start(), calls=%async_computation | async-start | bytes 3932160 | tf_op jit(solution)/shard_map/psum | solution.py:95
  8.4 18.5 %collective-permute-start.3 = (f32[8,8,1,720]{3,1,0,2:T(8,128)}, f32[8,8,1,720]{3,1,0,2:T(8,128)}, u32[]{:S(2)}, u32[]{:S(2)}) collective-permute-start(f32[8,8,1,720]{3,1,0,2:T(8,128)} %get-tuple-element.14), channel_id=1, source_target_pairs={{1,0},{2,1},{3,2},{4,3},{5,4},{6,5},{7,6},{9,8},{10,9},{11,10},{12... | collective-permute-start | bytes 552968 | tf_op jit(solution)/shard_map/ppermute | solution.py:27
  9.7 17.2 %collective-permute-start.4 = (f32[8,8,1,720]{3,1,0,2:T(8,128)}, f32[8,8,1,720]{3,1,0,2:T(8,128)}, u32[]{:S(2)}, u32[]{:S(2)}) collective-permute-start(f32[8,8,1,720]{3,1,0,2:T(8,128)} %get-tuple-element.15), channel_id=1, source_target_pairs={{0,1},{1,2},{2,3},{3,4},{4,5},{5,6},{6,7},{8,9},{9,10},{10,11},{11... | collective-permute-start | bytes 552968 | tf_op jit(solution)/shard_map/ppermute | solution.py:24
  13.4 13.5 %collective-permute-start.2 = (f32[8,8,720]{2,1,0:T(8,128)}, f32[8,8,720]{2,1,0:T(8,128)}, u32[]{:S(2)}, u32[]{:S(2)}) collective-permute-start(f32[8,8,720]{2,1,0:T(8,128)} %get-tuple-element.16), channel_id=1, source_target_pairs={{16,0},{24,8},{0,16},{8,24},{17,1},{25,9},{1,17},{9,25},{18,2},{26... | collective-permute-start | bytes 552968 | tf_op jit(solution)/shard_map/ppermute | solution.py:14
  18.7 7.2 %collective-permute-start.1 = (f32[8,8,30,1]{2,1,3,0:T(8,128)S(1)}, f32[8,8,30,1]{2,1,3,0:T(8,128)S(1)}, u32[]{:S(2)}, u32[]{:S(2)}) collective-permute-start(f32[8,8,30,1]{2,1,3,0:T(8,128)S(1)} %copy.31), channel_id=1, source_target_pairs={{0,8},{8,16},{16,24},{24,0},{1,9},{9,17},{17,25},{25,1},{2,10},{10... | collective-permute-start | bytes 23048 | tf_op jit(solution)/shard_map/ppermute | solution.py:24
  20.7 4.2 %collective-permute-start = (f32[8,8,30,1]{2,1,3,0:T(8,128)S(1)}, f32[8,8,30,1]{2,1,3,0:T(8,128)S(1)}, u32[]{:S(2)}, u32[]{:S(2)}) collective-permute-start(f32[8,8,30,1]{2,1,3,0:T(8,128)S(1)} %copy.30), channel_id=1, source_target_pairs={{8,0},{16,8},{24,16},{0,24},{9,1},{17,9},{25,17},{1,25},{10,2},{18... | collective-permute-start | bytes 23048 | tf_op jit(solution)/shard_map/ppermute | solution.py:27
  26.9 5.3 %slice-start = ((s8[5898240]{0:T(1024)(128)(4,1)}), s8[4194304]{0:T(1024)(128)(4,1)S(1)}, s32[]{:S(2)}) async-start(s8[5898240]{0:T(1024)(128)(4,1)} %bitcast.35), calls=%async_computation.1 | async-start | bytes 8388608
  28.3 3.9 %slice-start.1 = ((s8[5898240]{0:T(1024)(128)(4,1)}), s8[1703936]{0:T(1024)(128)(4,1)S(1)}, s32[]{:S(2)}) async-start(s8[5898240]{0:T(1024)(128)(4,1)} %bitcast.35), calls=%async_computation.2 | async-start | bytes 3407872
  32.2 3.6 %copy-start.1 = (f32[1,8,30,720]{3,1,0,2:T(8,128)}, f32[1,8,30,720]{3,1,0,2:T(8,128)S(1)}, u32[]{:S(2)}) copy-start(f32[1,8,30,720]{3,1,0,2:T(8,128)S(1)} %get-tuple-element.11) | copy-start | bytes 2073604
  32.2 5.4 %copy-start.2 = (f32[720,128]{1,0:T(8,128)S(1)}, f32[720,128]{1,0:T(8,128)}, u32[]{:S(2)}) copy-start(f32[720,128]{1,0:T(8,128)} %get-tuple-element.19) | copy-start | bytes 1105924
  32.2 5.4 %copy-start.4 = (f32[720,128]{1,0:T(8,128)S(1)}, f32[720,128]{1,0:T(8,128)}, u32[]{:S(2)}) copy-start(f32[720,128]{1,0:T(8,128)} %get-tuple-element.20) | copy-start | bytes 1105924
  35.8 1.8 %copy-start = (f32[5,8,30,720]{3,1,0,2:T(8,128)}, f32[5,8,30,720]{3,1,0,2:T(8,128)S(1)}, u32[]{:S(2)}) copy-start(f32[5,8,30,720]{3,1,0,2:T(8,128)S(1)} %fusion.10) | copy-start | bytes 10368004
  37.6 6.4 %copy-start.7 = (s32[30]{0:T(128)S(1)}, s32[30]{0:T(128)}, u32[]{:S(2)}) copy-start(s32[30]{0:T(128)} %param.4) | copy-start | bytes 364
  37.6 6.4 %copy-start.6 = (s32[30]{0:T(128)S(1)}, s32[30]{0:T(128)}, u32[]{:S(2)}) copy-start(s32[30]{0:T(128)} %param.5) | copy-start | bytes 364
  37.6 74.9 %copy-start.3 = (f32[720,128]{1,0:T(8,128)S(1)}, f32[720,128]{1,0:T(8,128)}, u32[]{:S(2)}) copy-start(f32[720,128]{1,0:T(8,128)} %get-tuple-element.19) | copy-start | bytes 1105924
  37.6 74.9 %copy-start.5 = (f32[720,128]{1,0:T(8,128)S(1)}, f32[720,128]{1,0:T(8,128)}, u32[]{:S(2)}) copy-start(f32[720,128]{1,0:T(8,128)} %get-tuple-element.20) | copy-start | bytes 1105924
Sparse Core Ops, SparseCore 0:
  44.1 68.3 all-reduce.1
where the time goes:
time: 135 us; the launch traced here: 134 us
  waiting for transfers between devices  68.4 us (51%)
  matrix products  18.3 us (14%)
  between operations  13.6 us (10%)
  other arithmetic  13.3 us (10%)
  starting transfers between devices  11 us (8%)
  local copies, waits for them, and re-layouts  9.88 us (7%)
    psum x1, waiting for transfers between devices, shards(): spec = lax.psum(spec, 'lon')  68.4 us
    dot_general x1, matrix products, shards(): jnp.einsum('frk,ck->frc', spec * weights[None], table, precision=lax.Prec...  11.9 us
    dot_general x1, matrix products, shards(): jnp.einsum('frc,ck->frk', flat, table, precision=lax.Precision.HIGHEST)  6.34 us
    ppermute x2, starting transfers between devices, with_halo(): lax.ppermute(lax.slice_in_dim(block, block.shape[dim] - width, None, axis...  5.24 us
    neg x1, other arithmetic, tendencies(): -((east[1] - west[1]) / (2.0 * dlon) + (cos_north * north[2] - cos_south...  3.87 us
    neg x1, other arithmetic, tendencies(): -((east[1] * east[3:] - west[1] * west[3:]) / (2.0 * dlon) + (cos_north *...  3.5 us
    add x1, local copies, waits for them, and re-layouts, shards(): return fields + step * filtered  3.16 us
    ppermute x1, starting transfers between devices, passed_along(): return lax.ppermute(block, axis, route)  2.97 us
  transfers between devices with their start and end apart: 6, of which 1 were waited for; matrix products, arithmetic and copies ran while one was open for 6% of the time, Pallas kernels for 0%

commit v1 on v0

v1 whole, which is shorter than its diff:
```python
import functools
import math

import jax
import jax.numpy as jnp
import ml_dtypes
import numpy as np
from jax import lax
from jax.experimental import pallas as pl
from jax.experimental.pallas import tpu as pltpu
from jax.sharding import PartitionSpec as P

KMAX = 128
F32, BF16 = jnp.float32, jnp.bfloat16
NT = (((1,), (1,)), ((), ()))
NN = (((1,), (0,)), ((), ()))
TN = (((0,), (0,)), ((), ()))


def split_np(a):
    hi = a.astype(ml_dtypes.bfloat16)
    lo = (a - hi.astype(np.float64)).astype(ml_dtypes.bfloat16)
    return hi, lo


def split(a):
    hi = a.astype(BF16)
    return hi, (a - hi.astype(F32)).astype(BF16)


def dot(a, b, dims):
    return lax.dot_general(a, b, dims, preferred_element_type=F32)


@functools.lru_cache(maxsize=None)
def factors(nlon, width):
    source, target, ranks = [], [], []
    for off in range(1, nlon // width):
        gaps = np.array(
            [1.0 / (nlon * math.sin((off * width + d) * math.pi / nlon)) for d in range(1 - width, width)]
        )
        idx = np.arange(width)
        rest = gaps[idx[:, None] - idx[None, :] + width - 1]
        bias = 1.0 + 1e-6 * idx[:, None] / width
        src, tgt = [], []
        while len(src) % 8 or not src or np.abs(rest).max() > 1e-9:
            i, j = np.unravel_index(np.argmax(np.abs(rest) * bias), rest.shape)
            row, col = rest[i] / rest[i, j], rest[:, j].copy()
            src.append(row)
            tgt.append(col)
            rest = rest - col[:, None] * row[None, :]
        ranks.append(len(src))
        source += src
        target += tgt
    return np.stack(source), np.stack(target), tuple(ranks)


def first_kernel(ranks, a, b, f_ref, side_ref, low_ref, high_ref, cos_ref, c_ref, s_ref, u_ref, t_ref, *rest):
    h_refs, w = rest[:-1], rest[-1]
    nf, rows, lon = f_ref.shape[0], f_ref.shape[2], f_ref.shape[3]
    frame, wide = w.shape[1], w.shape[2]
    for f in range(nf):
        w[f, 1 : rows + 1, 0:lon] = f_ref[f, 0]
        w[f, 0:1, 0:lon] = low_ref[0, f : f + 1]
        w[f, rows + 1 : rows + 2, 0:lon] = high_ref[0, f : f + 1]
        w[f, :, lon:wide] = side_ref[0, f]

    def dx(z):
        return pltpu.roll(z, wide - 1, 1) - pltpu.roll(z, 1, 1)

    def dy(z):
        return pltpu.roll(z, frame - 1, 0) - pltpu.roll(z, 1, 0)

    ua = w[1] * (-a)
    cv = w[2] * (cos_ref[:, 0:1] * (-b))
    tend = [dx(ua) + dy(cv), dx(w[0]) * (-a), dy(w[0]) * (-b)]
    for f in range(3, nf):
        tend.append(dx(ua * w[f]) + dy(cv * w[f]))
    parts = []
    for table in (c_ref[...], s_ref[...]):
        pairs = [split(t * table) for t in tend]
        hi = jnp.concatenate([p[0] for p in pairs], axis=0)
        lo = jnp.concatenate([p[1] for p in pairs], axis=0)
        n = u_ref.shape[0] // 2
        both = dot(u_ref[...], hi, NT)
        parts.append(both[:n] + both[n:] + dot(u_ref[0:n], lo, NT))
    for f in range(nf):
        t_ref[f, 0] = tend[f][:, 0:lon]
    at = 0
    for h_ref, r in zip(h_refs, ranks):
        h_ref[0, 0:r] = parts[0][at : at + r]
        h_ref[0, r : 2 * r] = parts[1][at : at + r]
        at += r


def second_kernel(ranks, f_ref, t_ref, c_ref, s_ref, keep_ref, wt_ref, thi, tlo, ihi, ilo, v_ref, *rest):
    h_refs, o_ref = rest[:-1], rest[-1]
    nf, rows, lon = f_ref.shape[0], f_ref.shape[2], f_ref.shape[3]
    frame = t_ref.shape[2]
    tend = jnp.concatenate([t_ref[f, 0] for f in range(nf)], axis=0)
    hi, lo = split(tend)
    spec = dot(hi, thi[...], NN) + dot(hi, tlo[...], NN) + dot(lo, thi[...], NN)
    spec = jnp.concatenate(
        [spec[f * frame : (f + 1) * frame] * wt_ref[...] for f in range(nf)], axis=0
    )
    hi, lo = split(spec)
    local = dot(hi, ihi[...], NN) + dot(hi, ilo[...], NN) + dot(lo, ihi[...], NN)
    far = []
    for part in range(2):
        h = jnp.concatenate([ref[0, part * r : (part + 1) * r] for ref, r in zip(h_refs, ranks)], axis=0)
        h = jnp.concatenate([h, jnp.zeros((v_ref.shape[0] // 3 - h.shape[0], h.shape[1]), F32)], axis=0) if v_ref.shape[0] // 3 > h.shape[0] else h
        hi, lo = split(h)
        far.append(dot(jnp.concatenate([hi, lo, hi], axis=0), v_ref[...], TN))
    for f in range(nf):
        at = slice(f * frame, (f + 1) * frame)
        add = local[at] + far[0][at] * s_ref[...] - far[1][at] * c_ref[...] + t_ref[f, 0] * keep_ref[:, 0:1]
        o_ref[f, 0] = f_ref[f, 0] + add[1 : rows + 1]


def shards(fields, mask, cutoff):
    nf, nlev, rows, lon = fields.shape
    lon_count = lax.axis_size("lon")
    lat_count = lax.axis_size("lat")
    nlon, nlat = lon * lon_count, rows * lat_count
    dlon, dlat = 2.0 * math.pi / nlon, math.pi / nlat
    step = 0.4 * dlon
    lat_pos, lon_pos = lax.axis_index("lat"), lax.axis_index("lon")
    frame = -(-(rows + 2) // 8) * 8
    wide = -(-(lon + 2) // 128) * 128
    source, target, ranks = factors(nlon, lon)
    total = sum(ranks)
    padr = -(-total // 16) * 16

    index = jnp.arange(nf)
    signs = jnp.where((index == 1) | (index == 2), -1.0, 1.0).astype(F32)[None, :, None]
    first = jnp.transpose(fields[:, :, 0, :], (1, 0, 2))
    last = jnp.transpose(fields[:, :, -1, :], (1, 0, 2))
    up = [(i, i + 1) for i in range(lat_count - 1)]
    down = [(j, i) for i, j in up]

    def around(x, off):
        return lax.ppermute(x, "lon", [(i, (i + off) % lon_count) for i in range(lon_count)])

    across = around(jnp.where(lat_pos == 0, first, last), lon_count // 2) * signs
    low = jnp.where(lat_pos == 0, across, lax.ppermute(last, "lat", up))
    high = jnp.where(lat_pos == lat_count - 1, across, lax.ppermute(first, "lat", down))
    edge_w = jnp.transpose(fields[:, :, :, 0], (1, 0, 2))
    edge_e = jnp.transpose(fields[:, :, :, -1], (1, 0, 2))
    east = around(edge_w, -1)
    west = around(edge_e, 1)
    side_w = wide - lon
    lane = jnp.arange(side_w)
    pad = ((0, 0), (0, 0), (1, frame - rows - 1))
    east, west = jnp.pad(east, pad)[..., None], jnp.pad(west, pad)[..., None]
    side = jnp.where(lane == 0, east, jnp.where(lane == side_w - 1, west, 0.0))

    rowid = jnp.clip(lat_pos * rows + jnp.arange(frame) - 1, 0, nlat - 1)
    cosine = jnp.cos(-math.pi / 2 + (rowid.astype(F32) + 0.5) * dlat)
    cosine = jnp.broadcast_to(cosine[:, None], (frame, 128))
    vpad = (1, frame - rows - 1)
    cut = jnp.pad(cutoff, vpad, constant_values=1)
    on = jnp.pad(mask.astype(F32), vpad) * step
    cols = lon_pos * lon + jnp.arange(wide, dtype=jnp.int32)
    turn = ((2 * cut[:, None] - 1) * cols[None, :]) % (2 * nlon)
    phase = turn.astype(F32) * (math.pi / nlon)
    inside = (jnp.arange(wide) < lon).astype(F32)
    cphase, sphase = jnp.cos(phase) * inside, jnp.sin(phase) * inside
    con, son = cphase[:, :lon] * on[:, None], sphase[:, :lon] * on[:, None]
    keep = jnp.broadcast_to((step - on)[:, None], (frame, 128))
    wavenum = jnp.arange(KMAX)
    scale = jnp.where(wavenum == 0, 1.0 / nlon, 2.0 / nlon).astype(F32)
    weights = (wavenum[None, :] < cut[:, None]).astype(F32) * scale[None, :] * on[:, None]
    weights = jnp.concatenate([weights, weights], axis=1)

    u = np.zeros((padr, wide))
    u[:total, :lon] = source
    u = np.concatenate(split_np(u), axis=0)
    v = np.zeros((padr, lon))
    v[:total] = target
    vhi, vlo = split_np(v)
    flip, at = [], 0
    for off, r in zip(range(1, lon_count), ranks):
        flip.append(jnp.where(lon_pos >= off, 1.0, -1.0) * jnp.ones((r,)))
    flip = jnp.concatenate(flip + [jnp.ones((padr - total,))])
    flip = jnp.concatenate([flip] * 3).astype(BF16)[:, None]
    v = jnp.asarray(np.concatenate([vhi, vhi, vlo], axis=0)) * flip
    angle = (np.arange(lon)[:, None] * np.arange(KMAX)[None, :] % nlon) * (2.0 * math.pi / nlon)
    table = np.concatenate([np.cos(angle), np.sin(angle)], axis=1)
    thi, tlo = split_np(table)
    ihi, ilo = np.ascontiguousarray(thi.T), np.ascontiguousarray(tlo.T)

    def whole(x):
        return pl.BlockSpec(x.shape, lambda l: (0,) * x.ndim)

    def level(*shape):
        return pl.BlockSpec((1,) + shape, lambda l: (l,) + (0,) * len(shape))

    def by_level(r, c):
        return pl.BlockSpec((nf, 1, r, c), lambda l: (0, l, 0, 0))

    m = nf * frame
    params = pltpu.CompilerParams(vmem_limit_bytes=32 * 1024 * 1024)
    shared = [cosine, cphase, sphase, jnp.asarray(u)]
    out = pl.pallas_call(
        functools.partial(first_kernel, ranks, 1.0 / (2.0 * dlon), 1.0 / (2.0 * dlat)),
        grid=(nlev,),
        in_specs=[by_level(rows, lon), level(nf, frame, side_w), level(nf, lon), level(nf, lon)]
        + [whole(x) for x in shared],
        out_specs=[by_level(frame, lon)] + [level(2 * r, m) for r in ranks],
        out_shape=[jax.ShapeDtypeStruct((nf, nlev, frame, lon), F32)]
        + [jax.ShapeDtypeStruct((nlev, 2 * r, m), F32) for r in ranks],
        scratch_shapes=[pltpu.VMEM((nf, frame, wide), F32)],
        compiler_params=params,
        name="tendency",
    )(fields, side, low, high, *shared)
    tend, sent = out[0], out[1:]
    got = [around(h, off) for off, h in zip(range(1, lon_count), sent)]
    shared = [con, son, keep, weights, jnp.asarray(thi), jnp.asarray(tlo), jnp.asarray(ihi), jnp.asarray(ilo), v]
    return pl.pallas_call(
        functools.partial(second_kernel, ranks),
        grid=(nlev,),
        in_specs=[by_level(rows, lon), by_level(frame, lon)]
        + [whole(x) for x in shared]
        + [level(2 * r, m) for r in ranks],
        out_specs=by_level(rows, lon),
        out_shape=jax.ShapeDtypeStruct(fields.shape, F32),
        compiler_params=params,
        name="projection",
    )(fields, tend, *shared, *got)


def solution(mesh):
    placed = (P(None, None, "lat", "lon"), P("lat"), P("lat"))
    return jax.shard_map(
        shards, mesh=mesh, in_specs=placed, out_specs=P(None, None, "lat", "lon"), check_vma=False
    )
```

time: 135 us -> 75.2 us (0.56)
  waiting for transfers between devices: 68.4 us -> 12.3 us
  Pallas kernels: 0 us -> 23.4 us
  matrix products: 18.3 us -> 0 us
  between operations: 13.6 us -> 0.25 us
  local copies, waits for them, and re-layouts: 9.88 us -> 22.6 us
  other arithmetic: 13.3 us -> 2.84 us
  starting transfers between devices: 11 us -> 13.4 us
    psum x1 -> x0, waiting for transfers between devices: 68.4 us -> none  [shards(): spec = lax.psum(spec, 'lon')]
    pallas_call x0 -> x2, Pallas kernels: none -> 23.4 us  [the longest x1 14.7 us: shards(): pl.pallas_call(functools.partial(second_kernel, ranks), grid=(nlev,), in_...]
    dot_general x2 -> x0, matrix products: 18.3 us -> none  [the longest x1 11.9 us: shards(): jnp.einsum('frk,ck->frc', spec * weights[None], table, precision=lax.Prec...]
    ppermute x5 -> x8, waiting for transfers between devices: 0.01 us -> 12.3 us  [the longest x6 12.3 us: around(): lax.ppermute(x, 'lon', [(i, (i + off) % lon_count) for i in range(lon_cou...]
    unnamed x22 -> x27, local copies, waits for them, and re-layouts: 2.85 us -> 12.7 us
    neg x2 -> x0, other arithmetic: 7.37 us -> none  [the longest x1 3.87 us: tendencies(): -((east[1] - west[1]) / (2.0 * dlon) + (cos_north * north[2] - cos_south...]
    pallas_call x0 -> x1, local copies, waits for them, and re-layouts: none -> 5.91 us  [shards(): pl.pallas_call(functools.partial(second_kernel, ranks), grid=(nlev,), in_...]
    add x1 -> x0, local copies, waits for them, and re-layouts: 3.16 us -> none  [shards(): return fields + step * filtered]
  transfers between devices with their start and end apart: 6 -> 8, of which waited for: 1 -> 2; matrix products, arithmetic and copies ran while one was open for 6% -> 20% of each run, Pallas kernels for 0% -> 0%
where the time goes in v1:
time: 75.2 us; the launch traced here: 74.9 us
  Pallas kernels  23.4 us (31%)
  local copies, waits for them, and re-layouts  22.6 us (30%)
  starting transfers between devices  13.4 us (18%)
  waiting for transfers between devices  12.3 us (16%)
  other arithmetic  2.84 us (4%)
    pallas_call x1, Pallas kernels, shards(): pl.pallas_call(functools.partial(second_kernel, ranks), grid=(nlev,), in_...  14.7 us
    unnamed x27, local copies, waits for them, and re-layouts  12.7 us
    ppermute x6, waiting for transfers between devices, around(): lax.ppermute(x, 'lon', [(i, (i + off) % lon_count) for i in range(lon_cou...  12.3 us
    ppermute x6, starting transfers between devices, around(): lax.ppermute(x, 'lon', [(i, (i + off) % lon_count) for i in range(lon_cou...  9.08 us
    pallas_call x1, Pallas kernels, shards(): pl.pallas_call(functools.partial(first_kernel, ranks, 1.0 / (2.0 * dlon),...  8.71 us
    pallas_call x1, local copies, waits for them, and re-layouts, shards(): pl.pallas_call(functools.partial(second_kernel, ranks), grid=(nlev,), in_...  5.91 us
    ppermute x1, starting transfers between devices, shards(): low = jnp.where(lat_pos == 0, across, lax.ppermute(last, 'lat', up))  3.04 us
    slice x1, local copies, waits for them, and re-layouts, shards(): edge_w = jnp.transpose(fields[:, :, :, 0], (1, 0, 2))  1.83 us
  transfers between devices with their start and end apart: 8, of which 2 were waited for; matrix products, arithmetic and copies ran while one was open for 20% of the time, Pallas kernels for 0%

profile of v1, /device:TPU:0, one launch (start us, length us, event | category | flops | bytes accessed | tf_op | source)
XLA Modules:
  0.0 74.9 jit_solution(15014689143964935628)
XLA Ops:
  0.0 1.1 %fusion.6 = (f32[8,8,1,720]{3,1,2,0:T(8,128)S(1)}, f32[8,8,1,720]{3,1,2,0:T(8,128)S(1)}) fusion(f32[8,8,30,720]{3,1,2,0:T(8,128)} %param.9), kind=kLoop, calls=%fused_computation.32 | loop fusion | bytes 737280 | tf_op jit(solution)/shard_map/slice | solution.py:136
  1.2 1.3 %collective-permute-start.4 = (f32[8,8,720]{2,1,0:T(8,128)S(1)}, f32[8,8,720]{2,1,0:T(8,128)S(1)}, u32[]{:S(2)}, u32[]{:S(2)}) collective-permute-start(f32[8,8,720]{2,1,0:T(8,128)S(1)} %bitcast.20), channel_id=1, source_target_pairs={{1,0},{2,1},{3,2},{4,3},{5,4},{6,5},{7,6},{9,8},{10,9},{11,10},{12... | collective-permute-start | bytes 552968 | tf_op jit(solution)/shard_map/ppermute | solution.py:146
  2.5 3.0 %collective-permute-start.3 = (f32[8,8,720]{2,1,0:T(8,128)S(1)}, f32[8,8,720]{2,1,0:T(8,128)S(1)}, u32[]{:S(2)}, u32[]{:S(2)}) collective-permute-start(f32[8,8,720]{2,1,0:T(8,128)S(1)} %bitcast.21), channel_id=1, source_target_pairs={{0,1},{1,2},{2,3},{3,4},{4,5},{5,6},{6,7},{8,9},{9,10},{10,11},{11... | collective-permute-start | bytes 552968 | tf_op jit(solution)/shard_map/ppermute | solution.py:145
  5.7 3.0 %collective-permute-start.2 = (f32[8,8,720]{2,1,0:T(8,128)S(1)}, f32[8,8,720]{2,1,0:T(8,128)S(1)}, u32[]{:S(2)}, u32[]{:S(2)}) collective-permute-start(f32[8,8,720]{2,1,0:T(8,128)S(1)} %broadcast_select_fusion), channel_id=1, source_target_pairs={{0,16},{8,24},{16,0},{24,8},{1,17},{9,25},{17,1},{25,9},{2,18},{10... | collective-permute-start | bytes 552968 | tf_op jit(solution)/shard_map/ppermute | solution.py:142
  8.8 1.8 %fusion.7 = (f32[8,8,30,1]{3,1,2,0:T(8,128)S(1)}, f32[8,8,30,1]{3,1,2,0:T(8,128)S(1)}) fusion(f32[8,8,30,720]{3,1,2,0:T(8,128)} %param.9), kind=kLoop, calls=%fused_computation.33 | loop fusion | bytes 30720 | tf_op jit(solution)/shard_map/slice | solution.py:147
  10.6 0.5 copy.27
  11.1 1.5 %collective-permute-start.1 = (f32[8,8,30]{2,0,1:T(8,128)S(1)}, f32[8,8,30]{2,0,1:T(8,128)}, u32[]{:S(2)}, u32[]{:S(2)}) collective-permute-start(f32[8,8,30]{2,0,1:T(8,128)S(1)} %bitcast.23), channel_id=1, source_target_pairs={{0,8},{8,16},{16,24},{24,0},{1,9},{9,17},{17,25},{25,1},{2,10},{10... | collective-permute-start | bytes 23048 | tf_op jit(solution)/shard_map/ppermute | solution.py:142
  13.1 1.5 %collective-permute-start = (f32[8,8,30]{2,0,1:T(8,128)S(1)}, f32[8,8,30]{2,0,1:T(8,128)}, u32[]{:S(2)}, u32[]{:S(2)}) collective-permute-start(f32[8,8,30]{2,0,1:T(8,128)S(1)} %bitcast.22), channel_id=1, source_target_pairs={{0,24},{8,0},{16,8},{24,16},{1,25},{9,1},{17,9},{25,17},{2,26},{10... | collective-permute-start | bytes 23048 | tf_op jit(solution)/shard_map/ppermute | solution.py:142
  14.7 0.6 fusion.8
  15.6 0.5 sine_multiply_fusion
  16.2 0.6 add_cosine_fusion
  16.7 7.1 %copy.24.f_ref = f32[8,8,30,720]{3,2,1,0:T(8,128)} copy(f32[8,8,30,720]{3,1,2,0:T(8,128)} %param.9) | data formatting | bytes 11059200 | tf_op args[0]
  23.9 0.9 %copy.31 = f32[8,8,30]{2,1,0:T(8,128)S(1)} copy(f32[8,8,30]{2,0,1:T(8,128)} %collective-permute-done.1) | data formatting | bytes 15360
  24.9 0.8 %copy.30 = f32[8,8,30]{2,1,0:T(8,128)S(1)} copy(f32[8,8,30]{2,0,1:T(8,128)} %collective-permute-done) | data formatting | bytes 15360
  25.7 0.6 select_select_fusion.side_ref
  26.5 0.7 broadcast_in_dim.79.cos_ref
  27.2 2.8 %copy-done = f32[8,8,30,720]{3,2,1,0:T(8,128)S(1)} copy-done((f32[8,8,30,720]{3,2,1,0:T(8,128)S(1)}, f32[8,8,30,720]{3,2,1,0:T(8,128)}, u32[]{:S(2)}) %copy-start) | copy-done | bytes 5529624
  30.0 8.7 %tendency.1 = (f32[8,8,32,720]{3,2,1,0:T(8,128)S(1)}, f32[8,32,256]{2,1,0:T(8,128)S(1)}, f32[8,16,256]{2,1,0:T(8,128)S(1)}, f32[8,32,256]{2,1,0:T(8,128)S(1)}) custom-call(f32[8,8,30,720]{3,2,1,0:T(8,128)S(1)} %copy-done, f32[8,8,32,48]{3,2,1,0:T(8,128)S(1)} %select_select_fusion.side_ref, f32[8,8,720]{2,1,0:T(8,128)S(1)} %get-tuple-element.18.low_ref, ...), custom_call_target="tpu_custom_call" | custom-call | tf_op jit(solution)/shard_map/tendency/pallas_call | solution.py:204
  38.8 1.1 %collective-permute-start.5 = (f32[8,32,256]{2,1,0:T(8,128)S(1)}, f32[8,32,256]{2,1,0:T(8,128)S(1)}, u32[]{:S(2)}, u32[]{:S(2)}) collective-permute-start(f32[8,32,256]{2,1,0:T(8,128)S(1)} %get-tuple-element.10), channel_id=1, source_target_pairs={{0,8},{8,16},{16,24},{24,0},{1,9},{9,17},{17,25},{25,1},{2,10},{10... | collective-permute-start | bytes 786440 | tf_op jit(solution)/shard_map/ppermute | solution.py:142
  39.9 1.9 %collective-permute-start.7 = (f32[8,32,256]{2,1,0:T(8,128)S(1)}, f32[8,32,256]{2,1,0:T(8,128)S(1)}, u32[]{:S(2)}, u32[]{:S(2)}) collective-permute-start(f32[8,32,256]{2,1,0:T(8,128)S(1)} %get-tuple-element.12), channel_id=1, source_target_pairs={{0,24},{8,0},{16,8},{24,16},{1,25},{9,1},{17,9},{25,17},{2,26},{10... | collective-permute-start | bytes 786440 | tf_op jit(solution)/shard_map/ppermute | solution.py:142
  41.8 8.3 %collective-permute-done.6.rest_1_ = f32[8,16,256]{2,1,0:T(8,128)S(1)} collective-permute-done((f32[8,16,256]{2,1,0:T(8,128)S(1)}, f32[8,16,256]{2,1,0:T(8,128)S(1)}, u32[]{:S(2)}, u32[]{:S(2)}) %collective-permute-start.6) | collective-permute-done | bytes 131104 | tf_op jit(solution)/shard_map/ppermute | solution.py:142
  50.1 4.0 %collective-permute-done.7.rest_2_ = f32[8,32,256]{2,1,0:T(8,128)S(1)} collective-permute-done((f32[8,32,256]{2,1,0:T(8,128)S(1)}, f32[8,32,256]{2,1,0:T(8,128)S(1)}, u32[]{:S(2)}, u32[]{:S(2)}) %collective-permute-start.7) | collective-permute-done | bytes 262176 | tf_op jit(solution)/shard_map/ppermute | solution.py:142
  54.3 14.7 %projection.1 = f32[8,8,30,720]{3,2,1,0:T(8,128)S(1)} custom-call(f32[8,8,30,720]{3,2,1,0:T(8,128)S(1)} %copy-done, f32[8,8,32,720]{3,2,1,0:T(8,128)S(1)} %get-tuple-element.9.t_ref, f32[32,720]{1,0:T(8,128)S(1)} %get-tuple-element.26.c_ref, f32[32,720]{1,0:T(8,128)S(1)} %get-tuple-element.25.s_ref, f32[32,128]{1,0:T(8,128)S(1)} %broadcast_in_dim.80.keep_ref, ...), custom_call_target="tpu_custom_call" | custom-call | tf_op jit(solution)/shard_map/projection/pallas_call | solution.py:219
  69.0 5.9 %copy.25 = f32[8,8,30,720]{3,1,2,0:T(8,128)} copy(f32[8,8,30,720]{3,2,1,0:T(8,128)S(1)} %projection.1) | data formatting | bytes 11059200 | tf_op jit(solution)/shard_map/projection/pallas_call | solution.py:219
  (50 shorter events, 1.7 us)
Async XLA Ops:
  0.0 15.5 %copy-start.6 = (bf16[144,720]{1,0:T(8,128)(2,1)S(1)}, bf16[144,720]{1,0:T(8,128)(2,1)}, u32[]{:S(2)}) copy-start(bf16[144,720]{1,0:T(8,128)(2,1)} %constant.85.clone) | copy-start | bytes 622084
  0.0 14.6 %copy-start.8 = (s32[30]{0:T(128)S(1)}, s32[30]{0:T(128)}, u32[]{:S(2)}) copy-start(s32[30]{0:T(128)} %param.10) | copy-start | bytes 364
  0.0 14.7 %copy-start.9 = (s32[30]{0:T(128)S(1)}, s32[30]{0:T(128)}, u32[]{:S(2)}) copy-start(s32[30]{0:T(128)} %param.11) | copy-start | bytes 364
  1.2 25.2 %collective-permute-start.4 = (f32[8,8,720]{2,1,0:T(8,128)S(1)}, f32[8,8,720]{2,1,0:T(8,128)S(1)}, u32[]{:S(2)}, u32[]{:S(2)}) collective-permute-start(f32[8,8,720]{2,1,0:T(8,128)S(1)} %bitcast.20), channel_id=1, source_target_pairs={{1,0},{2,1},{3,2},{4,3},{5,4},{6,5},{7,6},{9,8},{10,9},{11,10},{12... | collective-permute-start | bytes 552968 | tf_op jit(solution)/shard_map/ppermute | solution.py:146
  2.5 23.8 %collective-permute-start.3 = (f32[8,8,720]{2,1,0:T(8,128)S(1)}, f32[8,8,720]{2,1,0:T(8,128)S(1)}, u32[]{:S(2)}, u32[]{:S(2)}) collective-permute-start(f32[8,8,720]{2,1,0:T(8,128)S(1)} %bitcast.21), channel_id=1, source_target_pairs={{0,1},{1,2},{2,3},{3,4},{4,5},{5,6},{6,7},{8,9},{9,10},{10,11},{11... | collective-permute-start | bytes 552968 | tf_op jit(solution)/shard_map/ppermute | solution.py:145
  5.7 20.6 %collective-permute-start.2 = (f32[8,8,720]{2,1,0:T(8,128)S(1)}, f32[8,8,720]{2,1,0:T(8,128)S(1)}, u32[]{:S(2)}, u32[]{:S(2)}) collective-permute-start(f32[8,8,720]{2,1,0:T(8,128)S(1)} %broadcast_select_fusion), channel_id=1, source_target_pairs={{0,16},{8,24},{16,0},{24,8},{1,17},{9,25},{17,1},{25,9},{2,18},{10... | collective-permute-start | bytes 552968 | tf_op jit(solution)/shard_map/ppermute | solution.py:142
  11.1 12.8 %collective-permute-start.1 = (f32[8,8,30]{2,0,1:T(8,128)S(1)}, f32[8,8,30]{2,0,1:T(8,128)}, u32[]{:S(2)}, u32[]{:S(2)}) collective-permute-start(f32[8,8,30]{2,0,1:T(8,128)S(1)} %bitcast.23), channel_id=1, source_target_pairs={{0,8},{8,16},{16,24},{24,0},{1,9},{9,17},{17,25},{25,1},{2,10},{10... | collective-permute-start | bytes 23048 | tf_op jit(solution)/shard_map/ppermute | solution.py:142
  13.1 11.8 %collective-permute-start = (f32[8,8,30]{2,0,1:T(8,128)S(1)}, f32[8,8,30]{2,0,1:T(8,128)}, u32[]{:S(2)}, u32[]{:S(2)}) collective-permute-start(f32[8,8,30]{2,0,1:T(8,128)S(1)} %bitcast.22), channel_id=1, source_target_pairs={{0,24},{8,0},{16,8},{24,16},{1,25},{9,1},{17,9},{25,17},{2,26},{10... | collective-permute-start | bytes 23048 | tf_op jit(solution)/shard_map/ppermute | solution.py:142
  16.7 10.5 %copy-start.5 = (bf16[96,768]{1,0:T(8,128)(2,1)S(1)}, bf16[96,768]{1,0:T(8,128)(2,1)}, u32[]{:S(2)}) copy-start(bf16[96,768]{1,0:T(8,128)(2,1)} %constant.86.clone.u_ref) | copy-start | bytes 442372
  23.9 30.4 %copy-start.1 = (bf16[256,720]{1,0:T(8,128)(2,1)S(1)}, bf16[256,720]{1,0:T(8,128)(2,1)}, u32[]{:S(2)}) copy-start(bf16[256,720]{1,0:T(8,128)(2,1)} %constant.90.clone.ilo) | copy-start | bytes 1105924
  23.9 30.4 %copy-start.2 = (bf16[256,720]{1,0:T(8,128)(2,1)S(1)}, bf16[256,720]{1,0:T(8,128)(2,1)}, u32[]{:S(2)}) copy-start(bf16[256,720]{1,0:T(8,128)(2,1)} %constant.89.clone.ihi) | copy-start | bytes 1105924
  23.9 30.4 %copy-start.3 = (bf16[720,256]{1,0:T(8,128)(2,1)S(1)}, bf16[720,256]{1,0:T(8,128)(2,1)}, u32[]{:S(2)}) copy-start(bf16[720,256]{1,0:T(8,128)(2,1)} %constant.88.clone.tlo) | copy-start | bytes 1105924
  23.9 30.4 %copy-start.4 = (bf16[720,256]{1,0:T(8,128)(2,1)S(1)}, bf16[720,256]{1,0:T(8,128)(2,1)}, u32[]{:S(2)}) copy-start(bf16[720,256]{1,0:T(8,128)(2,1)} %constant.87.clone.thi) | copy-start | bytes 1105924
  23.9 17.9 %copy-start.7 = (s32[32]{0:T(128)S(1)}, s32[32]{0:T(128)}, u32[]{:S(2)}) copy-start(s32[32]{0:T(128)} %get-tuple-element.21) | copy-start | bytes 388
  27.2 2.8 %copy-start = (f32[8,8,30,720]{3,2,1,0:T(8,128)S(1)}, f32[8,8,30,720]{3,2,1,0:T(8,128)}, u32[]{:S(2)}) copy-start(f32[8,8,30,720]{3,2,1,0:T(8,128)} %copy.24.f_ref) | copy-start | bytes 16588804
  38.7 11.4 %collective-permute-start.6 = (f32[8,16,256]{2,1,0:T(8,128)S(1)}, f32[8,16,256]{2,1,0:T(8,128)S(1)}, u32[]{:S(2)}, u32[]{:S(2)}) collective-permute-start(f32[8,16,256]{2,1,0:T(8,128)S(1)} %get-tuple-element.11), channel_id=1, source_target_pairs={{0,16},{8,24},{16,0},{24,8},{1,17},{9,25},{17,1},{25,9},{2,18},{10... | collective-permute-start | bytes 393224 | tf_op jit(solution)/shard_map/ppermute | solution.py:142
  38.8 11.3 %collective-permute-start.5 = (f32[8,32,256]{2,1,0:T(8,128)S(1)}, f32[8,32,256]{2,1,0:T(8,128)S(1)}, u32[]{:S(2)}, u32[]{:S(2)}) collective-permute-start(f32[8,32,256]{2,1,0:T(8,128)S(1)} %get-tuple-element.10), channel_id=1, source_target_pairs={{0,8},{8,16},{16,24},{24,0},{1,9},{9,17},{17,25},{25,1},{2,10},{10... | collective-permute-start | bytes 786440 | tf_op jit(solution)/shard_map/ppermute | solution.py:142
  39.9 14.3 %collective-permute-start.7 = (f32[8,32,256]{2,1,0:T(8,128)S(1)}, f32[8,32,256]{2,1,0:T(8,128)S(1)}, u32[]{:S(2)}, u32[]{:S(2)}) collective-permute-start(f32[8,32,256]{2,1,0:T(8,128)S(1)} %get-tuple-element.12), channel_id=1, source_target_pairs={{0,24},{8,0},{16,8},{24,16},{1,25},{9,1},{17,9},{25,17},{2,26},{10... | collective-permute-start | bytes 786440 | tf_op jit(solution)/shard_map/ppermute | solution.py:142

commit v2 on v1

v2 whole, which is shorter than its diff:
```python
import functools
import math

import jax
import jax.numpy as jnp
import ml_dtypes
import numpy as np
from jax import lax
from jax.experimental import pallas as pl
from jax.experimental.pallas import tpu as pltpu
from jax.sharding import PartitionSpec as P

KMAX = 128
F32, BF16 = jnp.float32, jnp.bfloat16
NT = (((1,), (1,)), ((), ()))
NN = (((1,), (0,)), ((), ()))
TN = (((0,), (0,)), ((), ()))


def split_np(a):
    hi = a.astype(ml_dtypes.bfloat16)
    lo = (a - hi.astype(np.float64)).astype(ml_dtypes.bfloat16)
    return hi, lo


def split(a):
    hi = a.astype(BF16)
    return hi, (a - hi.astype(F32)).astype(BF16)


def dot(a, b, dims):
    return lax.dot_general(a, b, dims, preferred_element_type=F32)


@functools.lru_cache(maxsize=None)
def factors(nlon, width):
    source, target, ranks = [], [], []
    for off in range(1, nlon // width):
        gaps = np.array(
            [1.0 / (nlon * math.sin((off * width + d) * math.pi / nlon)) for d in range(1 - width, width)]
        )
        idx = np.arange(width)
        rest = gaps[idx[:, None] - idx[None, :] + width - 1]
        bias = 1.0 + 1e-6 * idx[:, None] / width
        src, tgt = [], []
        while len(src) % 8 or not src or np.abs(rest).max() > 1e-9:
            i, j = np.unravel_index(np.argmax(np.abs(rest) * bias), rest.shape)
            row, col = rest[i] / rest[i, j], rest[:, j].copy()
            src.append(row)
            tgt.append(col)
            rest = rest - col[:, None] * row[None, :]
        ranks.append(len(src))
        source += src
        target += tgt
    return np.stack(source), np.stack(target), tuple(ranks)


def per_level(table, nlev):
    return jnp.concatenate(
        [jnp.broadcast_to(table[r : r + 1], (nlev, table.shape[1])) for r in range(table.shape[0])], axis=0
    )


def first_kernel(
    ranks, a, b, f_ref, prev_ref, next_ref, low_ref, high_ref, east_ref, west_ref,
    cos_ref, c_ref, s_ref, u_ref, t_ref, *rest
):
    h_refs, w = rest[:-1], rest[-1]
    nf, chunk, nlev, lon = f_ref.shape
    wide = w.shape[3]
    here, steps = pl.program_id(0), pl.num_programs(0)
    flat = (chunk * nlev, wide)

    @pl.when(here == 0)
    def _():
        w[:, :, :, lon:wide] = jnp.zeros((nf, chunk + 2, nlev, wide - lon), F32)

    for f in range(nf):
        w[f, 1 : chunk + 1, :, 0:lon] = f_ref[f]
        w[f, 0, :, 0:lon] = jnp.where(here == 0, low_ref[f], prev_ref[f, 0])
        w[f, chunk + 1, :, 0:lon] = jnp.where(here == steps - 1, high_ref[f], next_ref[f, 0])
        for r in range(chunk):
            k = f * chunk + r
            w[f, r + 1, :, lon : lon + 1] = east_ref[0, :, k : k + 1]
            w[f, r + 1, :, wide - 1 : wide] = west_ref[0, :, k : k + 1]

    def mid(f):
        return w[f, 1 : chunk + 1].reshape(flat)

    def dx(z):
        return pltpu.roll(z, wide - 1, 1) - pltpu.roll(z, 1, 1)

    def dy(z):
        return (z[2:] - z[:-2]).reshape(flat)

    ua = mid(1) * (-a)
    cv = w[2] * (cos_ref[0][:, :, 0:1] * (-b))
    tend = [dx(ua) + dy(cv), dx(mid(0)) * (-a), dy(w[0]) * (-b)]
    for f in range(3, nf):
        tend.append(dx(ua * mid(f)) + dy(cv * w[f]))
    parts = []
    for table in (per_level(c_ref[0], nlev), per_level(s_ref[0], nlev)):
        pairs = [split(t * table) for t in tend]
        hi = jnp.concatenate([p[0] for p in pairs], axis=0)
        lo = jnp.concatenate([p[1] for p in pairs], axis=0)
        n = u_ref.shape[0] // 2
        both = dot(u_ref[...], hi, NT)
        parts.append(both[:n] + both[n:] + dot(u_ref[0:n], lo, NT))
    for f in range(nf):
        t_ref[f] = tend[f][:, 0:lon].reshape(chunk, nlev, lon)
    at = 0
    for h_ref, r in zip(h_refs, ranks):
        h_ref[0, 0:r] = parts[0][at : at + r]
        h_ref[0, r : 2 * r] = parts[1][at : at + r]
        at += r


def second_kernel(ranks, f_ref, t_ref, c_ref, s_ref, keep_ref, wt_ref, thi, tlo, ihi, ilo, v_ref, *rest):
    h_refs, o_ref = rest[:-1], rest[-1]
    nf, chunk, nlev, lon = f_ref.shape
    m = chunk * nlev
    tend = [t_ref[f].reshape(m, lon) for f in range(nf)]
    hi, lo = split(jnp.concatenate(tend, axis=0))
    spec = dot(hi, thi[...], NN) + dot(hi, tlo[...], NN) + dot(lo, thi[...], NN)
    wt = per_level(wt_ref[0], nlev)
    spec = jnp.concatenate([spec[f * m : (f + 1) * m] * wt for f in range(nf)], axis=0)
    hi, lo = split(spec)
    local = dot(hi, ihi[...], NN) + dot(hi, ilo[...], NN) + dot(lo, ihi[...], NN)
    far = []
    spare = v_ref.shape[0] // 3 - sum(ranks)
    for part in range(2):
        h = [ref[0, part * r : (part + 1) * r] for ref, r in zip(h_refs, ranks)]
        if spare:
            h.append(jnp.zeros((spare, nf * m), F32))
        hi, lo = split(jnp.concatenate(h, axis=0))
        far.append(dot(jnp.concatenate([hi, lo, hi], axis=0), v_ref[...], TN))
    c, s, keep = (per_level(x[0], nlev) for x in (c_ref, s_ref, keep_ref))
    for f in range(nf):
        at = slice(f * m, (f + 1) * m)
        add = local[at] + far[0][at] * s - far[1][at] * c + tend[f] * keep
        o_ref[f] = f_ref[f] + add.reshape(chunk, nlev, lon)


def shards(fields, mask, cutoff):
    fields = jnp.transpose(fields, (0, 2, 1, 3))
    nf, rows, nlev, lon = fields.shape
    chunk = max(c for c in range(1, 7) if rows % c == 0)
    steps = rows // chunk
    lon_count = lax.axis_size("lon")
    lat_count = lax.axis_size("lat")
    nlon, nlat = lon * lon_count, rows * lat_count
    dlon, dlat = 2.0 * math.pi / nlon, math.pi / nlat
    step = 0.4 * dlon
    lat_pos, lon_pos = lax.axis_index("lat"), lax.axis_index("lon")
    wide = -(-(lon + 2) // 128) * 128
    source, target, ranks = factors(nlon, lon)
    total = sum(ranks)
    padr = -(-total // 16) * 16

    index = jnp.arange(nf)
    signs = jnp.where((index == 1) | (index == 2), -1.0, 1.0).astype(F32)[:, None, None]
    first = fields[:, 0]
    last = fields[:, -1]
    up = [(i, i + 1) for i in range(lat_count - 1)]
    down = [(j, i) for i, j in up]

    def around(x, off):
        return lax.ppermute(x, "lon", [(i, (i + off) % lon_count) for i in range(lon_count)])

    across = around(jnp.where(lat_pos == 0, first, last), lon_count // 2) * signs
    low = jnp.where(lat_pos == 0, across, lax.ppermute(last, "lat", up))
    high = jnp.where(lat_pos == lat_count - 1, across, lax.ppermute(first, "lat", down))

    def columns(x):
        return x.reshape(nf, steps, chunk, nlev).transpose(1, 3, 0, 2).reshape(steps, nlev, nf * chunk)

    east = around(columns(fields[:, :, :, 0]), -1)
    west = around(columns(fields[:, :, :, -1]), 1)

    rowid = np.arange(steps)[:, None] * chunk + np.arange(chunk + 2)[None, :] - 1
    rowid = jnp.clip(lat_pos * rows + rowid, 0, nlat - 1)
    cosine = jnp.cos(-math.pi / 2 + (rowid.astype(F32) + 0.5) * dlat)
    cosine = jnp.broadcast_to(cosine[:, :, None, None], (steps, chunk + 2, nlev, 128))
    cut = cutoff.reshape(steps, chunk)
    on = mask.astype(F32).reshape(steps, chunk) * step
    cols = lon_pos * lon + jnp.arange(wide, dtype=jnp.int32)
    turn = ((2 * cut[:, :, None] - 1) * cols) % (2 * nlon)
    phase = turn.astype(F32) * (math.pi / nlon)
    inside = (jnp.arange(wide) < lon).astype(F32)
    cphase, sphase = jnp.cos(phase) * inside, jnp.sin(phase) * inside
    con, son = cphase[:, :, :lon] * on[:, :, None], sphase[:, :, :lon] * on[:, :, None]
    keep = jnp.broadcast_to((step - on)[:, :, None], (steps, chunk, lon))
    wavenum = jnp.arange(KMAX)
    scale = jnp.where(wavenum == 0, 1.0 / nlon, 2.0 / nlon).astype(F32)
    weights = (wavenum < cut[:, :, None]).astype(F32) * scale * on[:, :, None]
    weights = jnp.concatenate([weights, weights], axis=2)

    u = np.zeros((padr, wide))
    u[:total, :lon] = source
    u = np.concatenate(split_np(u), axis=0)
    v = np.zeros((padr, lon))
    v[:total] = target
    vhi, vlo = split_np(v)
    flip, at = [], 0
    for off, r in zip(range(1, lon_count), ranks):
        flip.append(jnp.where(lon_pos >= off, 1.0, -1.0) * jnp.ones((r,)))
    flip = jnp.concatenate(flip + [jnp.ones((padr - total,))])
    flip = jnp.concatenate([flip] * 3).astype(BF16)[:, None]
    v = jnp.asarray(np.concatenate([vhi, vhi, vlo], axis=0)) * flip
    angle = (np.arange(lon)[:, None] * np.arange(KMAX)[None, :] % nlon) * (2.0 * math.pi / nlon)
    table = np.concatenate([np.cos(angle), np.sin(angle)], axis=1)
    thi, tlo = split_np(table)
    ihi, ilo = np.ascontiguousarray(thi.T), np.ascontiguousarray(tlo.T)

    def whole(x):
        return pl.BlockSpec(x.shape, lambda i: (0,) * x.ndim)

    def stage(*shape):
        return pl.BlockSpec((1,) + shape, lambda i: (i,) + (0,) * len(shape))

    band = pl.BlockSpec((nf, chunk, nlev, lon), lambda i: (0, i, 0, 0))
    before = pl.BlockSpec((nf, 1, nlev, lon), lambda i: (0, jnp.maximum(i * chunk - 1, 0), 0, 0))
    after = pl.BlockSpec((nf, 1, nlev, lon), lambda i: (0, jnp.minimum(i * chunk + chunk, rows - 1), 0, 0))
    m = nf * chunk * nlev
    params = pltpu.CompilerParams(vmem_limit_bytes=32 * 1024 * 1024)
    u = jnp.asarray(u)
    out = pl.pallas_call(
        functools.partial(first_kernel, ranks, 1.0 / (2.0 * dlon), 1.0 / (2.0 * dlat)),
        grid=(steps,),
        in_specs=[band, before, after, whole(low), whole(high)]
        + [stage(nlev, nf * chunk)] * 2
        + [stage(chunk + 2, nlev, 128), stage(chunk, wide), stage(chunk, wide), whole(u)],
        out_specs=[band] + [stage(2 * r, m) for r in ranks],
        out_shape=[jax.ShapeDtypeStruct(fields.shape, F32)]
        + [jax.ShapeDtypeStruct((steps, 2 * r, m), F32) for r in ranks],
        scratch_shapes=[pltpu.VMEM((nf, chunk + 2, nlev, wide), F32)],
        compiler_params=params,
        name="tendency",
    )(fields, fields, fields, low, high, east, west, cosine, cphase, sphase, u)
    tend, sent = out[0], out[1:]
    got = [around(h, off) for off, h in zip(range(1, lon_count), sent)]
    shared = [jnp.asarray(x) for x in (thi, tlo, ihi, ilo)] + [v]
    out = pl.pallas_call(
        functools.partial(second_kernel, ranks),
        grid=(steps,),
        in_specs=[band, band, stage(chunk, lon), stage(chunk, lon), stage(chunk, lon), stage(chunk, 2 * KMAX)]
        + [whole(x) for x in shared]
        + [stage(2 * r, m) for r in ranks],
        out_specs=band,
        out_shape=jax.ShapeDtypeStruct(fields.shape, F32),
        compiler_params=params,
        name="projection",
    )(fields, tend, con, son, keep, weights, *shared, *got)
    return jnp.transpose(out, (0, 2, 1, 3))


def solution(mesh):
    placed = (P(None, None, "lat", "lon"), P("lat"), P("lat"))
    return jax.shard_map(
        shards, mesh=mesh, in_specs=placed, out_specs=P(None, None, "lat", "lon"), check_vma=False
    )
```

time: 75.2 us -> 60.9 us (0.81)
  local copies, waits for them, and re-layouts: 22.6 us -> 10.5 us
  Pallas kernels: 23.4 us -> 21.8 us
    unnamed x27 -> x20, local copies, waits for them, and re-layouts: 12.7 us -> 2.7 us
    pallas_call x1 -> x0, local copies, waits for them, and re-layouts: 5.91 us -> none  [shards(): pl.pallas_call(functools.partial(second_kernel, ranks), grid=(nlev,), in_...]
    slice x2 -> x3, local copies, waits for them, and re-layouts: 2.92 us -> 4.77 us  [the longest x2 3.31 us: shards(): west = around(columns(fields[:, :, :, -1]), 1)]
    squeeze x0 -> x1, local copies, waits for them, and re-layouts: none -> 1.72 us  [shards(): first = fields[:, 0]]
    pallas_call x1, Pallas kernels: 14.7 us -> 13.6 us  [shards(): pl.pallas_call(functools.partial(second_kernel, ranks), grid=(steps,), in...]
    select_n x1, other arithmetic: 0.12 us -> 1.11 us  [shards(): jnp.where(lat_pos == 0, first, last)]
  transfers between devices with their start and end apart: 8 -> 8, of which waited for: 2 -> 3; matrix products, arithmetic and copies ran while one was open for 20% -> 14% of each run, Pallas kernels for 0% -> 0%
where the time goes in v2:
time: 60.9 us; the launch traced here: 60.6 us
  Pallas kernels  21.8 us (36%)
  starting transfers between devices  13.9 us (23%)
  waiting for transfers between devices  12 us (20%)
  local copies, waits for them, and re-layouts  10.5 us (17%)
  other arithmetic  2.15 us (4%)
    pallas_call x1, Pallas kernels, shards(): pl.pallas_call(functools.partial(second_kernel, ranks), grid=(steps,), in...  13.6 us
    ppermute x6, waiting for transfers between devices, around(): lax.ppermute(x, 'lon', [(i, (i + off) % lon_count) for i in range(lon_cou...  12 us
    ppermute x6, starting transfers between devices, around(): lax.ppermute(x, 'lon', [(i, (i + off) % lon_count) for i in range(lon_cou...  9.6 us
    pallas_call x1, Pallas kernels, shards(): pl.pallas_call(functools.partial(first_kernel, ranks, 1.0 / (2.0 * dlon),...  8.16 us
    slice x2, local copies, waits for them, and re-layouts, shards(): west = around(columns(fields[:, :, :, -1]), 1)  3.31 us
    ppermute x1, starting transfers between devices, shards(): low = jnp.where(lat_pos == 0, across, lax.ppermute(last, 'lat', up))  3.04 us
    unnamed x20, local copies, waits for them, and re-layouts  2.7 us
    squeeze x1, local copies, waits for them, and re-layouts, shards(): first = fields[:, 0]  1.72 us
  transfers between devices with their start and end apart: 8, of which 3 were waited for; matrix products, arithmetic and copies ran while one was open for 14% of the time, Pallas kernels for 0%

profile of v2, /device:TPU:0, one launch (start us, length us, event | category | flops | bytes accessed | tf_op | source)
XLA Modules:
  0.0 60.6 jit_solution(4348139803503256690)
XLA Ops:
  0.0 1.1 %broadcast_select_fusion = f32[8,8,720]{2,1,0:T(8,128)S(1)} fusion(pred[]{:T(512)S(6)} %eq.33, f32[8,30,8,720]{3,2,1,0:T(8,128)} %bitcast.22), kind=kLoop, calls=%fused_computation.16 | loop fusion | flops 46080 | bytes 552961 | tf_op jit(solution)/shard_map/jit(_where)/select_n | solution.py:170
  1.1 3.1 %collective-permute-start = (f32[8,8,720]{2,1,0:T(8,128)S(1)}, f32[8,8,720]{2,1,0:T(8,128)S(1)}, u32[]{:S(2)}, u32[]{:S(2)}) collective-permute-start(f32[8,8,720]{2,1,0:T(8,128)S(1)} %broadcast_select_fusion), channel_id=1, source_target_pairs={{0,16},{8,24},{16,0},{24,8},{1,17},{9,25},{17,1},{25,9},{2,18},{10... | collective-permute-start | bytes 552968 | tf_op jit(solution)/shard_map/ppermute | solution.py:168
  4.2 1.7 %slice_bitcast_fusion.1 = (f32[8,8,720]{2,1,0:T(8,128)}, f32[8,8,720]{2,1,0:T(8,128)S(1)}) fusion(f32[8,30,8,720]{3,2,1,0:T(8,128)} %bitcast.23), kind=kLoop, calls=%fused_computation.1 | loop fusion | bytes 737280 | tf_op jit(solution)/shard_map/squeeze | solution.py:162
  5.9 1.3 %collective-permute-start.2 = (f32[8,8,720]{2,1,0:T(8,128)}, f32[8,8,720]{2,1,0:T(8,128)S(1)}, u32[]{:S(2)}, u32[]{:S(2)}) collective-permute-start(f32[8,8,720]{2,1,0:T(8,128)} %get-tuple-element.15), channel_id=1, source_target_pairs={{1,0},{2,1},{3,2},{4,3},{5,4},{6,5},{7,6},{9,8},{10,9},{11,10},{12... | collective-permute-start | bytes 552968 | tf_op jit(solution)/shard_map/ppermute | solution.py:172
  7.2 3.0 %collective-permute-start.1 = (f32[8,8,720]{2,1,0:T(8,128)S(1)}, f32[8,8,720]{2,1,0:T(8,128)S(1)}, u32[]{:S(2)}, u32[]{:S(2)}) collective-permute-start(f32[8,8,720]{2,1,0:T(8,128)S(1)} %get-tuple-element.16), channel_id=1, source_target_pairs={{0,1},{1,2},{2,3},{3,4},{4,5},{5,6},{6,7},{8,9},{9,10},{10,11},{11... | collective-permute-start | bytes 552968 | tf_op jit(solution)/shard_map/ppermute | solution.py:171
  10.3 1.8 %fusion.6 = (f32[8,30,8,1]{3,2,1,0:T(8,128)S(1)}, f32[8,30,8,1]{3,2,1,0:T(8,128)S(1)}) fusion(f32[8,30,8,720]{3,2,1,0:T(8,128)} %bitcast.24), kind=kLoop, calls=%fused_computation.29 | loop fusion | bytes 30720 | tf_op jit(solution)/shard_map/slice | solution.py:178
  12.1 1.5 %copy.17 = f32[8,30,8,1]{2,0,1,3:T(8,128)S(1)} copy(f32[8,30,8,1]{3,2,1,0:T(8,128)S(1)} %get-tuple-element.13) | data formatting | bytes 15360 | tf_op jit(solution)/shard_map/slice | solution.py:178
  13.6 0.3 copy.18
  13.9 0.1 reshape.101
  14.0 1.5 %collective-permute-start.4 = (f32[5,8,48]{2,1,0:T(8,128)S(1)}, f32[5,8,48]{2,1,0:T(8,128)S(1)}, u32[]{:S(2)}, u32[]{:S(2)}) collective-permute-start(f32[5,8,48]{2,1,0:T(8,128)S(1)} %reshape.101), channel_id=1, source_target_pairs={{0,8},{8,16},{16,24},{24,0},{1,9},{9,17},{17,25},{25,1},{2,10},{10... | collective-permute-start | bytes 23048 | tf_op jit(solution)/shard_map/ppermute | solution.py:168
  15.6 1.5 %copy.15 = f32[8,30,8,1]{2,0,1,3:T(8,128)S(1)} copy(f32[8,30,8,1]{3,2,1,0:T(8,128)S(1)} %get-tuple-element.14) | data formatting | bytes 15360 | tf_op jit(solution)/shard_map/slice | solution.py:177
  17.0 0.3 copy.16
  17.4 0.1 reshape.100
  17.5 1.5 %collective-permute-start.3 = (f32[5,8,48]{2,1,0:T(8,128)S(1)}, f32[5,8,48]{2,1,0:T(8,128)S(1)}, u32[]{:S(2)}, u32[]{:S(2)}) collective-permute-start(f32[5,8,48]{2,1,0:T(8,128)S(1)} %reshape.100), channel_id=1, source_target_pairs={{0,24},{8,0},{16,8},{24,16},{1,25},{9,1},{17,9},{25,17},{2,26},{10... | collective-permute-start | bytes 23048 | tf_op jit(solution)/shard_map/ppermute | solution.py:168
  19.5 0.6 sine_multiply_fusion
  20.4 1.0 %collective-permute-done.3.east_ref = f32[5,8,48]{2,1,0:T(8,128)S(1)} collective-permute-done((f32[5,8,48]{2,1,0:T(8,128)S(1)}, f32[5,8,48]{2,1,0:T(8,128)S(1)}, u32[]{:S(2)}, u32[]{:S(2)}) %collective-permute-start.3) | collective-permute-done | bytes 7712 | tf_op jit(solution)/shard_map/ppermute | solution.py:168
  21.6 2.7 %copy-done = f32[8,8,30,720]{3,1,2,0:T(8,128)S(1)} copy-done((f32[8,8,30,720]{3,1,2,0:T(8,128)S(1)}, f32[8,8,30,720]{3,1,2,0:T(8,128)}, u32[]{:S(2)}) %copy-start) | copy-done | bytes 5529624
  24.3 8.2 %tendency.1 = (f32[8,30,8,720]{3,2,1,0:T(8,128)S(1)}, f32[5,32,384]{2,1,0:T(8,128)S(1)}, f32[5,16,384]{2,1,0:T(8,128)S(1)}, f32[5,32,384]{2,1,0:T(8,128)S(1)}) custom-call(f32[8,30,8,720]{3,2,1,0:T(8,128)S(1)} %bitcast.25, f32[8,30,8,720]{3,2,1,0:T(8,128)S(1)} %bitcast.26, f32[8,30,8,720]{3,2,1,0:T(8,128)S(1)} %bitcast.27, ...), custom_call_target="tpu_custom_call" | custom-call | tf_op jit(solution)/shard_map/tendency/pallas_call | solution.py:227
  32.4 0.6 collective-permute-start.6
  33.0 2.4 %collective-permute-start.5 = (f32[5,32,384]{2,1,0:T(8,128)S(1)}, f32[5,32,384]{2,1,0:T(8,128)S(1)}, u32[]{:S(2)}, u32[]{:S(2)}) collective-permute-start(f32[5,32,384]{2,1,0:T(8,128)S(1)} %get-tuple-element.10), channel_id=1, source_target_pairs={{0,8},{8,16},{16,24},{24,0},{1,9},{9,17},{17,25},{25,1},{2,10},{10... | collective-permute-start | bytes 737288 | tf_op jit(solution)/shard_map/ppermute | solution.py:168
  35.4 0.5 collective-permute-start.7
  35.9 7.1 %collective-permute-done.6.rest_1_ = f32[5,16,384]{2,1,0:T(8,128)S(1)} collective-permute-done((f32[5,16,384]{2,1,0:T(8,128)S(1)}, f32[5,16,384]{2,1,0:T(8,128)S(1)}, u32[]{:S(2)}, u32[]{:S(2)}) %collective-permute-start.6) | collective-permute-done | bytes 122912 | tf_op jit(solution)/shard_map/ppermute | solution.py:168
  43.0 3.9 %collective-permute-done.7.rest_2_ = f32[5,32,384]{2,1,0:T(8,128)S(1)} collective-permute-done((f32[5,32,384]{2,1,0:T(8,128)S(1)}, f32[5,32,384]{2,1,0:T(8,128)S(1)}, u32[]{:S(2)}, u32[]{:S(2)}) %collective-permute-start.7) | collective-permute-done | bytes 245792 | tf_op jit(solution)/shard_map/ppermute | solution.py:168
  47.0 13.6 %projection.1 = f32[8,30,8,720]{3,2,1,0:T(8,128)} custom-call(f32[8,30,8,720]{3,2,1,0:T(8,128)S(1)} %bitcast.28, f32[8,30,8,720]{3,2,1,0:T(8,128)S(1)} %get-tuple-element.9.t_ref, f32[5,6,720]{2,1,0:T(8,128)S(1)} %get-tuple-element.22.c_ref, f32[5,6,720]{2,1,0:T(8,128)S(1)} %get-tuple-element.21.s_ref, f32[5,6,720]{2,1,0:T(8,128)S(1)} %broadcast_in_dim.25.keep_ref, ...), custom_call_target="tpu_custom_call" | custom-call | tf_op jit(solution)/shard_map/projection/pallas_call | solution.py:243
  (46 shorter events, 0.9 us)
Async XLA Ops:
  0.0 19.4 %copy-start.6 = (bf16[144,720]{1,0:T(8,128)(2,1)S(1)}, bf16[144,720]{1,0:T(8,128)(2,1)}, u32[]{:S(2)}) copy-start(bf16[144,720]{1,0:T(8,128)(2,1)} %constant.81.clone) | copy-start | bytes 622084
  0.0 20.2 %copy-start.7 = (s32[5,8]{1,0:T(8,128)S(1)}, s32[5,8]{1,0:T(8,128)}, u32[]{:S(2)}) copy-start(s32[5,8]{1,0:T(8,128)} %constant.80.clone) | copy-start | bytes 484
  0.0 21.6 %copy-start.5 = (bf16[96,768]{1,0:T(8,128)(2,1)S(1)}, bf16[96,768]{1,0:T(8,128)(2,1)}, u32[]{:S(2)}) copy-start(bf16[96,768]{1,0:T(8,128)(2,1)} %constant.82.clone.u_ref) | copy-start | bytes 442372
  0.0 19.0 %copy-start.9 = (s32[30]{0:T(128)S(1)}, s32[30]{0:T(128)}, u32[]{:S(2)}) copy-start(s32[30]{0:T(128)} %param.11) | copy-start | bytes 364
  0.0 19.1 %copy-start.8 = (s32[30]{0:T(128)S(1)}, s32[30]{0:T(128)}, u32[]{:S(2)}) copy-start(s32[30]{0:T(128)} %param.12) | copy-start | bytes 364
  1.1 19.2 %collective-permute-start = (f32[8,8,720]{2,1,0:T(8,128)S(1)}, f32[8,8,720]{2,1,0:T(8,128)S(1)}, u32[]{:S(2)}, u32[]{:S(2)}) collective-permute-start(f32[8,8,720]{2,1,0:T(8,128)S(1)} %broadcast_select_fusion), channel_id=1, source_target_pairs={{0,16},{8,24},{16,0},{24,8},{1,17},{9,25},{17,1},{25,9},{2,18},{10... | collective-permute-start | bytes 552968 | tf_op jit(solution)/shard_map/ppermute | solution.py:168
  5.9 14.4 %collective-permute-start.2 = (f32[8,8,720]{2,1,0:T(8,128)}, f32[8,8,720]{2,1,0:T(8,128)S(1)}, u32[]{:S(2)}, u32[]{:S(2)}) collective-permute-start(f32[8,8,720]{2,1,0:T(8,128)} %get-tuple-element.15), channel_id=1, source_target_pairs={{1,0},{2,1},{3,2},{4,3},{5,4},{6,5},{7,6},{9,8},{10,9},{11,10},{12... | collective-permute-start | bytes 552968 | tf_op jit(solution)/shard_map/ppermute | solution.py:172
  7.2 13.1 %collective-permute-start.1 = (f32[8,8,720]{2,1,0:T(8,128)S(1)}, f32[8,8,720]{2,1,0:T(8,128)S(1)}, u32[]{:S(2)}, u32[]{:S(2)}) collective-permute-start(f32[8,8,720]{2,1,0:T(8,128)S(1)} %get-tuple-element.16), channel_id=1, source_target_pairs={{0,1},{1,2},{2,3},{3,4},{4,5},{5,6},{6,7},{8,9},{9,10},{10,11},{11... | collective-permute-start | bytes 552968 | tf_op jit(solution)/shard_map/ppermute | solution.py:171
  14.0 6.4 %collective-permute-start.4 = (f32[5,8,48]{2,1,0:T(8,128)S(1)}, f32[5,8,48]{2,1,0:T(8,128)S(1)}, u32[]{:S(2)}, u32[]{:S(2)}) collective-permute-start(f32[5,8,48]{2,1,0:T(8,128)S(1)} %reshape.101), channel_id=1, source_target_pairs={{0,8},{8,16},{16,24},{24,0},{1,9},{9,17},{17,25},{25,1},{2,10},{10... | collective-permute-start | bytes 23048 | tf_op jit(solution)/shard_map/ppermute | solution.py:168
  17.5 4.0 %collective-permute-start.3 = (f32[5,8,48]{2,1,0:T(8,128)S(1)}, f32[5,8,48]{2,1,0:T(8,128)S(1)}, u32[]{:S(2)}, u32[]{:S(2)}) collective-permute-start(f32[5,8,48]{2,1,0:T(8,128)S(1)} %reshape.100), channel_id=1, source_target_pairs={{0,24},{8,0},{16,8},{24,16},{1,25},{9,1},{17,9},{25,17},{2,26},{10... | collective-permute-start | bytes 23048 | tf_op jit(solution)/shard_map/ppermute | solution.py:168
  21.6 2.7 %copy-start = (f32[8,8,30,720]{3,1,2,0:T(8,128)S(1)}, f32[8,8,30,720]{3,1,2,0:T(8,128)}, u32[]{:S(2)}) copy-start(f32[8,8,30,720]{3,1,2,0:T(8,128)} %param.10) | copy-start | bytes 16588804
  24.3 22.7 %copy-start.1 = (bf16[256,720]{1,0:T(8,128)(2,1)S(1)}, bf16[256,720]{1,0:T(8,128)(2,1)}, u32[]{:S(2)}) copy-start(bf16[256,720]{1,0:T(8,128)(2,1)} %constant.86.clone.ilo) | copy-start | bytes 1105924
  24.3 22.7 %copy-start.2 = (bf16[256,720]{1,0:T(8,128)(2,1)S(1)}, bf16[256,720]{1,0:T(8,128)(2,1)}, u32[]{:S(2)}) copy-start(bf16[256,720]{1,0:T(8,128)(2,1)} %constant.85.clone.ihi) | copy-start | bytes 1105924
  24.3 22.7 %copy-start.3 = (bf16[720,256]{1,0:T(8,128)(2,1)S(1)}, bf16[720,256]{1,0:T(8,128)(2,1)}, u32[]{:S(2)}) copy-start(bf16[720,256]{1,0:T(8,128)(2,1)} %constant.84.clone.tlo) | copy-start | bytes 1105924
  24.3 22.7 %copy-start.4 = (bf16[720,256]{1,0:T(8,128)(2,1)S(1)}, bf16[720,256]{1,0:T(8,128)(2,1)}, u32[]{:S(2)}) copy-start(bf16[720,256]{1,0:T(8,128)(2,1)} %constant.83.clone.thi) | copy-start | bytes 1105924
  32.4 10.6 %collective-permute-start.6 = (f32[5,16,384]{2,1,0:T(8,128)S(1)}, f32[5,16,384]{2,1,0:T(8,128)S(1)}, u32[]{:S(2)}, u32[]{:S(2)}) collective-permute-start(f32[5,16,384]{2,1,0:T(8,128)S(1)} %get-tuple-element.11), channel_id=1, source_target_pairs={{0,16},{8,24},{16,0},{24,8},{1,17},{9,25},{17,1},{25,9},{2,18},{10... | collective-permute-start | bytes 368648 | tf_op jit(solution)/shard_map/ppermute | solution.py:168
  33.0 10.0 %collective-permute-start.5 = (f32[5,32,384]{2,1,0:T(8,128)S(1)}, f32[5,32,384]{2,1,0:T(8,128)S(1)}, u32[]{:S(2)}, u32[]{:S(2)}) collective-permute-start(f32[5,32,384]{2,1,0:T(8,128)S(1)} %get-tuple-element.10), channel_id=1, source_target_pairs={{0,8},{8,16},{16,24},{24,0},{1,9},{9,17},{17,25},{25,1},{2,10},{10... | collective-permute-start | bytes 737288 | tf_op jit(solution)/shard_map/ppermute | solution.py:168
  35.4 11.5 %collective-permute-start.7 = (f32[5,32,384]{2,1,0:T(8,128)S(1)}, f32[5,32,384]{2,1,0:T(8,128)S(1)}, u32[]{:S(2)}, u32[]{:S(2)}) collective-permute-start(f32[5,32,384]{2,1,0:T(8,128)S(1)} %get-tuple-element.12), channel_id=1, source_target_pairs={{0,24},{8,0},{16,8},{24,16},{1,25},{9,1},{17,9},{25,17},{2,26},{10... | collective-permute-start | bytes 737288 | tf_op jit(solution)/shard_map/ppermute | solution.py:168

commit v3 on v2

--- a/solution.py
+++ b/solution.py
@@ -12,6 +12,7 @@
 
 KMAX = 128
 F32, BF16 = jnp.float32, jnp.bfloat16
+MESH = pl.DeviceIdType.MESH
 NT = (((1,), (1,)), ((), ()))
 NN = (((1,), (0,)), ((), ()))
 TN = (((0,), (0,)), ((), ()))
@@ -61,31 +62,114 @@
     )
 
 
-def first_kernel(
-    ranks, a, b, f_ref, prev_ref, next_ref, low_ref, high_ref, east_ref, west_ref,
-    cos_ref, c_ref, s_ref, u_ref, t_ref, *rest
-):
-    h_refs, w = rest[:-1], rest[-1]
-    nf, chunk, nlev, lon = f_ref.shape
+def first_kernel(ranks, a, b, chunk, f_any, cos_ref, c_ref, s_ref, u_ref, t_ref, *rest):
+    n_off = len(ranks)
+    got, (fv, w, halo, edge, ghost), held = rest[:n_off], rest[n_off : n_off + 5], rest[n_off + 5 : 2 * n_off + 5]
+    load_sem, row_send, row_recv, col_send, col_recv, far_send, far_recv = rest[2 * n_off + 5 :]
+    nf, rows, nlev, lon = fv.shape
     wide = w.shape[3]
-    here, steps = pl.program_id(0), pl.num_programs(0)
+    steps = rows // chunk
     flat = (chunk * nlev, wide)
-
-    @pl.when(here == 0)
-    def _():
-        w[:, :, :, lon:wide] = jnp.zeros((nf, chunk + 2, nlev, wide - lon), F32)
-
-    for f in range(nf):
-        w[f, 1 : chunk + 1, :, 0:lon] = f_ref[f]
-        w[f, 0, :, 0:lon] = jnp.where(here == 0, low_ref[f], prev_ref[f, 0])
-        w[f, chunk + 1, :, 0:lon] = jnp.where(here == steps - 1, high_ref[f], next_ref[f, 0])
-        for r in range(chunk):
-            k = f * chunk + r
-            w[f, r + 1, :, lon : lon + 1] = east_ref[0, :, k : k + 1]
-            w[f, r + 1, :, wide - 1 : wide] = west_ref[0, :, k : k + 1]
-
-    def mid(f):
-        return w[f, 1 : chunk + 1].reshape(flat)
+    lat_pos, lon_pos = lax.axis_index("lat"), lax.axis_index("lon")
+    lats, lons = lax.axis_size("lat"), lax.axis_size("lon")
+    opposite = lax.rem(lon_pos + lons // 2, lons)
+
+    def peer(off):
+        return lax.rem(lon_pos + off, lons)
+
+    load = pltpu.make_async_copy(f_any, fv, load_sem)
+    load.start()
+    barrier = pltpu.get_barrier_semaphore()
+
+    def greet(lat, lon_at):
+        pl.semaphore_signal(barrier, inc=1, device_id=(lon_at, lat), device_id_type=MESH)
+
+    for off in range(1, lons):
+        greet(lat_pos, peer(off))
+
+    @pl.when(lat_pos > 0)
+    def _():
+        greet(lat_pos - 1, lon_pos)
+
+    @pl.when(lat_pos < lats - 1)
+    def _():
+        greet(lat_pos + 1, lon_pos)
+
+    peers = lons - 1 + jnp.minimum(lat_pos, 1) + jnp.minimum(lats - 1 - lat_pos, 1)
+    pl.semaphore_wait(barrier, peers)
+
+    def row_copy(row, slot, lat, lon_at, which):
+        return pltpu.make_async_remote_copy(
+            src_ref=f_any.at[:, row],
+            dst_ref=halo.at[slot],
+            send_sem=row_send.at[which],
+            recv_sem=row_recv.at[slot],
+            device_id=(lon_at, lat),
+            device_id_type=MESH,
+        )
+
+    @pl.when(lat_pos > 0)
+    def _():
+        row_copy(0, 1, lat_pos - 1, lon_pos, 0).start()
+
+    @pl.when(lat_pos == 0)
+    def _():
+        row_copy(0, 0, lat_pos, opposite, 0).start()
+
+    @pl.when(lat_pos < lats - 1)
+    def _():
+        row_copy(rows - 1, 0, lat_pos + 1, lon_pos, 1).start()
+
+    @pl.when(lat_pos == lats - 1)
+    def _():
+        row_copy(rows - 1, 1, lat_pos, opposite, 1).start()
+
+    w[:, :, :, lon:wide] = jnp.zeros((nf, chunk + 2, nlev, wide - lon), F32)
+    lane = lax.broadcasted_iota(jnp.int32, (nlev, 128), 1)
+    load.wait()
+
+    def pack(i, carry):
+        west_edge = jnp.zeros((nlev, 128), F32)
+        east_edge = jnp.zeros((nlev, 128), F32)
+        for f in range(nf):
+            for r in range(chunk):
+                here = lane == f * chunk + r
+                west_edge = jnp.where(here, fv[f, i * chunk + r, :, 0:1], west_edge)
+                east_edge = jnp.where(here, fv[f, i * chunk + r, :, lon - 1 : lon], east_edge)
+        edge[0, i] = west_edge
+        edge[1, i] = east_edge
+        return carry
+
+    lax.fori_loop(0, steps, pack, 0)
+    cols = [
+        pltpu.make_async_remote_copy(
+            src_ref=edge.at[side],
+            dst_ref=ghost.at[side],
+            send_sem=col_send.at[side],
+            recv_sem=col_recv.at[side],
+            device_id=(peer(lons - 1 if side == 0 else 1), lat_pos),
+            device_id_type=MESH,
+        )
+        for side in range(2)
+    ]
+    for copy in cols:
+        copy.start()
+    for which in range(2):
+        row_copy(0, which, lat_pos, opposite, which).wait()
+    for copy in cols:
+        copy.wait()
+    turn_low = jnp.where(lat_pos == 0, -1.0, 1.0)
+    turn_high = jnp.where(lat_pos == lats - 1, -1.0, 1.0)
+
+    def far_copy(at, i):
+        return pltpu.make_async_remote_copy(
+            src_ref=held[at].at[i],
+            dst_ref=got[at].at[i],
+            send_sem=far_send.at[at, i],
+            recv_sem=far_recv.at[at, i],
+            device_id=(peer(at + 1), lat_pos),
+            device_id_type=MESH,
+        )
 
     def dx(z):
         return pltpu.roll(z, wide - 1, 1) - pltpu.roll(z, 1, 1)
@@ -93,26 +177,55 @@
     def dy(z):
         return (z[2:] - z[:-2]).reshape(flat)
 
-    ua = mid(1) * (-a)
-    cv = w[2] * (cos_ref[0][:, :, 0:1] * (-b))
-    tend = [dx(ua) + dy(cv), dx(mid(0)) * (-a), dy(w[0]) * (-b)]
-    for f in range(3, nf):
-        tend.append(dx(ua * mid(f)) + dy(cv * w[f]))
-    parts = []
-    for table in (per_level(c_ref[0], nlev), per_level(s_ref[0], nlev)):
-        pairs = [split(t * table) for t in tend]
-        hi = jnp.concatenate([p[0] for p in pairs], axis=0)
-        lo = jnp.concatenate([p[1] for p in pairs], axis=0)
-        n = u_ref.shape[0] // 2
-        both = dot(u_ref[...], hi, NT)
-        parts.append(both[:n] + both[n:] + dot(u_ref[0:n], lo, NT))
-    for f in range(nf):
-        t_ref[f] = tend[f][:, 0:lon].reshape(chunk, nlev, lon)
-    at = 0
-    for h_ref, r in zip(h_refs, ranks):
-        h_ref[0, 0:r] = parts[0][at : at + r]
-        h_ref[0, r : 2 * r] = parts[1][at : at + r]
-        at += r
+    def work(i, carry):
+        for f in range(nf):
+            below, above = halo[0, f], halo[1, f]
+            if f in (1, 2):
+                below, above = below * turn_low, above * turn_high
+            w[f, 1 : chunk + 1, :, 0:lon] = fv[f, pl.ds(i * chunk, chunk)]
+            w[f, 0, :, 0:lon] = jnp.where(i == 0, below, fv[f, jnp.maximum(i * chunk - 1, 0)])
+            w[f, chunk + 1, :, 0:lon] = jnp.where(
+                i == steps - 1, above, fv[f, jnp.minimum(i * chunk + chunk, rows - 1)]
+            )
+            for r in range(chunk):
+                k = f * chunk + r
+                w[f, r + 1, :, lon : lon + 1] = ghost[0, i, :, k : k + 1]
+                w[f, r + 1, :, wide - 1 : wide] = ghost[1, i, :, k : k + 1]
+
+        def mid(f):
+            return w[f, 1 : chunk + 1].reshape(flat)
+
+        ua = mid(1) * (-a)
+        cv = w[2] * (cos_ref[i][:, :, 0:1] * (-b))
+        tend = [dx(ua) + dy(cv), dx(mid(0)) * (-a), dy(w[0]) * (-b)]
+        for f in range(3, nf):
+            tend.append(dx(ua * mid(f)) + dy(cv * w[f]))
+        parts = []
+        for table in (per_level(c_ref[i], nlev), per_level(s_ref[i], nlev)):
+            pairs = [split(t * table) for t in tend]
+            hi = jnp.concatenate([p[0] for p in pairs], axis=0)
+            lo = jnp.concatenate([p[1] for p in pairs], axis=0)
+            n = u_ref.shape[0] // 2
+            both = dot(u_ref[...], hi, NT)
+            parts.append(both[:n] + both[n:] + dot(u_ref[0:n], lo, NT))
+        at = 0
+        for off, r in enumerate(ranks):
+            held[off][i, 0:r] = parts[0][at : at + r]
+            held[off][i, r : 2 * r] = parts[1][at : at + r]
+            far_copy(off, i).start()
+            at += r
+        for f in range(nf):
+            t_ref[f, pl.ds(i * chunk, chunk)] = tend[f][:, 0:lon].reshape(chunk, nlev, lon)
+        return carry
+
+    lax.fori_loop(0, steps, work, 0)
+
+    def finish(i, carry):
+        for off in range(n_off):
+            far_copy(off, i).wait()
+        return carry
+
+    lax.fori_loop(0, steps, finish, 0)
 
 
 def second_kernel(ranks, f_ref, t_ref, c_ref, s_ref, keep_ref, wt_ref, thi, tlo, ihi, ilo, v_ref, *rest):
@@ -157,26 +270,6 @@
     total = sum(ranks)
     padr = -(-total // 16) * 16
 
-    index = jnp.arange(nf)
-    signs = jnp.where((index == 1) | (index == 2), -1.0, 1.0).astype(F32)[:, None, None]
-    first = fields[:, 0]
-    last = fields[:, -1]
-    up = [(i, i + 1) for i in range(lat_count - 1)]
-    down = [(j, i) for i, j in up]
-
-    def around(x, off):
-        return lax.ppermute(x, "lon", [(i, (i + off) % lon_count) for i in range(lon_count)])
-
-    across = around(jnp.where(lat_pos == 0, first, last), lon_count // 2) * signs
-    low = jnp.where(lat_pos == 0, across, lax.ppermute(last, "lat", up))
-    high = jnp.where(lat_pos == lat_count - 1, across, lax.ppermute(first, "lat", down))
-
-    def columns(x):
-        return x.reshape(nf, steps, chunk, nlev).transpose(1, 3, 0, 2).reshape(steps, nlev, nf * chunk)
-
-    east = around(columns(fields[:, :, :, 0]), -1)
-    west = around(columns(fields[:, :, :, -1]), 1)
-
     rowid = np.arange(steps)[:, None] * chunk + np.arange(chunk + 2)[None, :] - 1
     rowid = jnp.clip(lat_pos * rows + rowid, 0, nlat - 1)
     cosine = jnp.cos(-math.pi / 2 + (rowid.astype(F32) + 0.5) * dlat)
@@ -219,26 +312,40 @@
         return pl.BlockSpec((1,) + shape, lambda i: (i,) + (0,) * len(shape))
 
     band = pl.BlockSpec((nf, chunk, nlev, lon), lambda i: (0, i, 0, 0))
-    before = pl.BlockSpec((nf, 1, nlev, lon), lambda i: (0, jnp.maximum(i * chunk - 1, 0), 0, 0))
-    after = pl.BlockSpec((nf, 1, nlev, lon), lambda i: (0, jnp.minimum(i * chunk + chunk, rows - 1), 0, 0))
     m = nf * chunk * nlev
     params = pltpu.CompilerParams(vmem_limit_bytes=32 * 1024 * 1024)
     u = jnp.asarray(u)
+    n_off = len(ranks)
+    vmem, far = pl.BlockSpec(memory_space=pltpu.VMEM), pl.BlockSpec(memory_space=pl.ANY)
     out = pl.pallas_call(
-        functools.partial(first_kernel, ranks, 1.0 / (2.0 * dlon), 1.0 / (2.0 * dlat)),
-        grid=(steps,),
-        in_specs=[band, before, after, whole(low), whole(high)]
-        + [stage(nlev, nf * chunk)] * 2
-        + [stage(chunk + 2, nlev, 128), stage(chunk, wide), stage(chunk, wide), whole(u)],
-        out_specs=[band] + [stage(2 * r, m) for r in ranks],
+        functools.partial(first_kernel, ranks, 1.0 / (2.0 * dlon), 1.0 / (2.0 * dlat), chunk),
+        in_specs=[far] + [vmem] * 4,
+        out_specs=[vmem] + [far] * n_off,
         out_shape=[jax.ShapeDtypeStruct(fields.shape, F32)]
         + [jax.ShapeDtypeStruct((steps, 2 * r, m), F32) for r in ranks],
-        scratch_shapes=[pltpu.VMEM((nf, chunk + 2, nlev, wide), F32)],
-        compiler_params=params,
+        scratch_shapes=[
+            pltpu.VMEM(fields.shape, F32),
+            pltpu.VMEM((nf, chunk + 2, nlev, wide), F32),
+            pltpu.VMEM((2, nf, nlev, lon), F32),
+            pltpu.VMEM((2, steps, nlev, 128), F32),
+            pltpu.VMEM((2, steps, nlev, 128), F32),
+        ]
+        + [pltpu.VMEM((steps, 2 * r, m), F32) for r in ranks]
+        + [
+            pltpu.SemaphoreType.DMA,
+            pltpu.SemaphoreType.DMA((2,)),
+            pltpu.SemaphoreType.DMA((2,)),
+            pltpu.SemaphoreType.DMA((2,)),
+            pltpu.SemaphoreType.DMA((2,)),
+            pltpu.SemaphoreType.DMA((n_off, steps)),
+            pltpu.SemaphoreType.DMA((n_off, steps)),
+        ],
+        compiler_params=pltpu.CompilerParams(
+            vmem_limit_bytes=48 * 1024 * 1024, collective_id=0, has_side_effects=True
+        ),
         name="tendency",
-    )(fields, fields, fields, low, high, east, west, cosine, cphase, sphase, u)
-    tend, sent = out[0], out[1:]
-    got = [around(h, off) for off, h in zip(range(1, lon_count), sent)]
+    )(fields, cosine, cphase, sphase, u)
+    tend, got = out[0], out[1:]
     shared = [jnp.asarray(x) for x in (thi, tlo, ihi, ilo)] + [v]
     out = pl.pallas_call(
         functools.partial(second_kernel, ranks),

time: 60.9 us -> 47.6 us (0.78)
  Pallas kernels: 21.8 us -> 39.1 us
  starting transfers between devices: 13.9 us -> 0 us
  waiting for transfers between devices: 12 us -> 0 us
  local copies, waits for them, and re-layouts: 10.5 us -> 4.69 us
  other arithmetic: 2.15 us -> 3.47 us
    pallas_call x1, Pallas kernels: 8.16 us -> 25.5 us  [shards(): pl.pallas_call(functools.partial(first_kernel, ranks, 1.0 / (2.0 * dlon),...]
    ppermute x8 -> x0, starting transfers between devices: 13.9 us -> none  [the longest x6 9.6 us: around(): lax.ppermute(x, 'lon', [(i, (i + off) % lon_count) for i in range(lon_cou...]
    ppermute x8 -> x0, waiting for transfers between devices: 12 us -> none  [the longest x6 12 us: around(): lax.ppermute(x, 'lon', [(i, (i + off) % lon_count) for i in range(lon_cou...]
    slice x3 -> x0, local copies, waits for them, and re-layouts: 4.77 us -> none  [the longest x2 3.31 us: shards(): west = around(columns(fields[:, :, :, -1]), 1)]
    squeeze x1 -> x0, local copies, waits for them, and re-layouts: 1.72 us -> none  [shards(): first = fields[:, 0]]
    select_n x3 -> x0, other arithmetic: 1.22 us -> none  [the longest x1 1.11 us: shards(): jnp.where(lat_pos == 0, first, last)]
    mul x1, other arithmetic: 0.09 us -> 1.18 us  [shards(): v = jnp.asarray(np.concatenate([vhi, vhi, vlo], axis=0)) * flip]
    unnamed x20 -> x14, local copies, waits for them, and re-layouts: 2.7 us -> 3.59 us
  transfers between devices with their start and end apart: 8 -> 0, of which waited for: 3 -> 0; matrix products, arithmetic and copies ran while one was open for 14% -> 0% of each run, Pallas kernels for 0% -> 0%
where the time goes in v3:
time: 47.6 us; the launch traced here: 47.4 us
  Pallas kernels  39.1 us (82%)
  local copies, waits for them, and re-layouts  4.69 us (10%)
  other arithmetic  3.47 us (7%)
    pallas_call x1, Pallas kernels, shards(): pl.pallas_call(functools.partial(first_kernel, ranks, 1.0 / (2.0 * dlon),...  25.5 us
    pallas_call x1, Pallas kernels, shards(): pl.pallas_call(functools.partial(second_kernel, ranks), grid=(steps,), in...  13.6 us
    unnamed x14, local copies, waits for them, and re-layouts  3.59 us
    mul x1, other arithmetic, shards(): v = jnp.asarray(np.concatenate([vhi, vhi, vlo], axis=0)) * flip  1.18 us

profile of v3, /device:TPU:0, one launch (start us, length us, event | category | flops | bytes accessed | tf_op | source)
XLA Modules:
  0.0 47.4 jit_solution(17035063403070474579)
XLA Ops:
  0.0 0.0 copy-start.2
  0.0 0.0 copy-start.3
  0.0 0.8 %convert_multiply_fusion = f32[30]{0:T(128)S(1)} fusion(s32[30]{0:T(128)} %param.11), kind=kLoop, calls=%fused_computation.22 | loop fusion | flops 60 | bytes 240 | tf_op jit(solution)/shard_map/mul | solution.py:278
  0.8 0.1 concatenate.17
  0.9 0.1 mul.129
  1.0 0.7 %add_cosine_fusion = f32[5,8]{1,0:T(8,128)S(1)} fusion(s32[5,8]{1,0:T(8,128)} %constant.76.clone, s32[]{:T(128)S(6)} %mul.115), kind=kLoop, calls=%fused_computation.18 | loop fusion | flops 240 | bytes 324 | tf_op jit(solution)/shard_map/cos | solution.py:275
  1.8 0.7 %broadcast_in_dim_reshape.4 = s32[5,6]{1,0:T(8,128)S(1)} reshape(s32[30]{0:T(128)} %param.12) | data formatting | bytes 240 | tf_op jit(solution)/shard_map/broadcast_in_dim;reshape | solution.py:280
  2.5 0.1 select_multiply_fusion
  2.6 0.1 broadcast_in_dim.11.keep_ref
  2.7 0.1 broadcast_in_dim.10.cos_ref
  2.8 1.2 %broadcast_multiply_fusion.v_ref = bf16[144,720]{1,0:T(8,128)(2,1)S(1)} fusion(bf16[144,720]{1,0:T(8,128)(2,1)} %constant.77.clone, bf16[144]{0:T(256)(128)(2,1)S(1)} %concatenate.17), kind=kLoop, calls=%fused_computation.11 | loop fusion | flops 103680 | bytes 415008 | tf_op jit(solution)/shard_map/mul | solution.py:302
  4.0 0.6 %sine_multiply_fusion = (f32[5,6,768]{2,1,0:T(8,128)S(1)}, f32[5,6,768]{2,1,0:T(8,128)S(1)}) fusion(f32[768]{0:T(1024)S(1)} %fusion.5, s32[768]{0:T(1024)S(1)} %iota_add_fusion, s32[5,6]{1,0:T(8,128)S(1)} %multiply_add_fusion), kind=kLoop, calls=%fused_computation.5 | loop fusion | flops 253440 | bytes 190584 | tf_op jit(solution)/shard_map/mul | solution.py:283
  4.6 0.1 slice_multiply_fusion
  4.7 0.0 copy-start.6
  4.7 0.9 %copy-done.6 = bf16[96,768]{1,0:T(8,128)(2,1)S(1)} copy-done((bf16[96,768]{1,0:T(8,128)(2,1)S(1)}, bf16[96,768]{1,0:T(8,128)(2,1)}, u32[]{:S(2)}) %copy-start.6) | copy-done | bytes 147480
  5.6 25.5 %tendency.1 = (f32[8,30,8,720]{3,2,1,0:T(8,128)}, f32[5,32,384]{2,1,0:T(8,128)S(1)}, f32[5,16,384]{2,1,0:T(8,128)S(1)}, f32[5,32,384]{2,1,0:T(8,128)S(1)}) custom-call(f32[8,30,8,720]{3,2,1,0:T(8,128)} %bitcast.2, f32[5,8,8,128]{3,2,1,0:T(8,128)S(1)} %broadcast_in_dim.10.cos_ref, f32[5,6,768]{2,1,0:T(8,128)S(1)} %get-tuple-element.14.c_ref, ...), custom_call_target="tpu_custom_call" | custom-call | tf_op jit(solution)/shard_map/tendency/pallas_call | solution.py:320
  31.1 0.0 copy-done.2
  31.1 0.0 copy-done.3
  31.1 0.0 copy-done.4
  31.1 0.0 copy-done.5
  31.1 0.0 copy-done
  31.2 0.0 copy-start.1
  31.2 2.7 %copy-done.1 = f32[8,30,8,720]{3,2,1,0:T(8,128)S(1)} copy-done((f32[8,30,8,720]{3,2,1,0:T(8,128)S(1)}, f32[8,30,8,720]{3,2,1,0:T(8,128)}, u32[]{:S(2)}) %copy-start.1) | copy-done | bytes 5529624
  33.8 13.6 %projection.1 = f32[8,30,8,720]{3,2,1,0:T(8,128)} custom-call(f32[8,30,8,720]{3,2,1,0:T(8,128)S(1)} %bitcast.3, f32[8,30,8,720]{3,2,1,0:T(8,128)S(1)} %copy-done.1, f32[5,6,720]{2,1,0:T(8,128)S(1)} %get-tuple-element.16.c_ref, f32[5,6,720]{2,1,0:T(8,128)S(1)} %get-tuple-element.15.s_ref, f32[5,6,720]{2,1,0:T(8,128)S(1)} %broadcast_in_dim.11.keep_ref, ...), custom_call_target="tpu_custom_call" | custom-call | tf_op jit(solution)/shard_map/projection/pallas_call | solution.py:350
  (13 shorter events, 0.0 us)
Async XLA Ops:
  0.0 31.1 %copy-start.2 = (bf16[256,720]{1,0:T(8,128)(2,1)S(1)}, bf16[256,720]{1,0:T(8,128)(2,1)}, u32[]{:S(2)}) copy-start(bf16[256,720]{1,0:T(8,128)(2,1)} %constant.82.clone.ilo) | copy-start | bytes 1105924
  0.0 31.1 %copy-start.3 = (bf16[256,720]{1,0:T(8,128)(2,1)S(1)}, bf16[256,720]{1,0:T(8,128)(2,1)}, u32[]{:S(2)}) copy-start(bf16[256,720]{1,0:T(8,128)(2,1)} %constant.81.clone.ihi) | copy-start | bytes 1105924
  0.0 31.1 %copy-start.4 = (bf16[720,256]{1,0:T(8,128)(2,1)S(1)}, bf16[720,256]{1,0:T(8,128)(2,1)}, u32[]{:S(2)}) copy-start(bf16[720,256]{1,0:T(8,128)(2,1)} %constant.80.clone.tlo) | copy-start | bytes 1105924
  0.0 31.1 %copy-start.5 = (bf16[720,256]{1,0:T(8,128)(2,1)S(1)}, bf16[720,256]{1,0:T(8,128)(2,1)}, u32[]{:S(2)}) copy-start(bf16[720,256]{1,0:T(8,128)(2,1)} %constant.79.clone.thi) | copy-start | bytes 1105924
  2.5 28.7 %copy-start = (f32[8,8,30,720]{3,1,2,0:T(8,128)S(1)}, f32[8,8,30,720]{3,1,2,0:T(8,128)}, u32[]{:S(2)}) copy-start(f32[8,8,30,720]{3,1,2,0:T(8,128)} %param.10) | copy-start | bytes 16588804
  4.7 0.9 %copy-start.6 = (bf16[96,768]{1,0:T(8,128)(2,1)S(1)}, bf16[96,768]{1,0:T(8,128)(2,1)}, u32[]{:S(2)}) copy-start(bf16[96,768]{1,0:T(8,128)(2,1)} %constant.78.clone.u_ref) | copy-start | bytes 442372
  31.2 2.7 %copy-start.1 = (f32[8,30,8,720]{3,2,1,0:T(8,128)S(1)}, f32[8,30,8,720]{3,2,1,0:T(8,128)}, u32[]{:S(2)}) copy-start(f32[8,30,8,720]{3,2,1,0:T(8,128)} %get-tuple-element.9.t_ref) | copy-start | bytes 16588804

commit v4 on v3

--- a/solution.py
+++ b/solution.py
@@ -62,7 +62,15 @@
     )
 
 
-def first_kernel(ranks, a, b, chunk, f_any, cos_ref, c_ref, s_ref, u_ref, t_ref, *rest):
+def polar(lat_pos, lats, rows, chunk, i):
+    nlat = lats * rows
+    start = lat_pos * rows + i * chunk
+    return (start < nlat // 6) | (start + chunk > nlat - nlat // 6)
+
+
+def first_kernel(
+    ranks, a, b, chunk, f_any, cos_ref, c_ref, s_ref, u_ref, keep_ref, wt_ref, thi, tlo, ihi, ilo, t_ref, *rest
+):
     n_off = len(ranks)
     got, (fv, w, halo, edge, ghost), held = rest[:n_off], rest[n_off : n_off + 5], rest[n_off + 5 : 2 * n_off + 5]
     load_sem, row_send, row_recv, col_send, col_recv, far_send, far_recv = rest[2 * n_off + 5 :]
@@ -210,48 +218,74 @@
             parts.append(both[:n] + both[n:] + dot(u_ref[0:n], lo, NT))
         at = 0
         for off, r in enumerate(ranks):
-            held[off][i, 0:r] = parts[0][at : at + r]
-            held[off][i, r : 2 * r] = parts[1][at : at + r]
-            far_copy(off, i).start()
+            turned = jnp.where(lon_pos + off + 1 >= lons, -1.0, 1.0)
+            held[off][i, 0:r] = parts[0][at : at + r] * turned
+            held[off][i, r : 2 * r] = parts[1][at : at + r] * turned
             at += r
+
+        @pl.when(polar(lat_pos, lats, rows, chunk, i))
+        def _():
+            for off in range(n_off):
+                far_copy(off, i).start()
+
         for f in range(nf):
             t_ref[f, pl.ds(i * chunk, chunk)] = tend[f][:, 0:lon].reshape(chunk, nlev, lon)
         return carry
 
     lax.fori_loop(0, steps, work, 0)
 
+    def local(i, carry):
+        m = chunk * nlev
+        tend = [t_ref[f, pl.ds(i * chunk, chunk)].reshape(m, lon) for f in range(nf)]
+        hi, lo = split(jnp.concatenate(tend, axis=0))
+        spec = dot(hi, thi[...], NN) + dot(hi, tlo[...], NN) + dot(lo, thi[...], NN)
+        wt = per_level(wt_ref[i], nlev)
+        spec = jnp.concatenate([spec[f * m : (f + 1) * m] * wt for f in range(nf)], axis=0)
+        hi, lo = split(spec)
+        proj = dot(hi, ihi[...], NN) + dot(hi, ilo[...], NN) + dot(lo, ihi[...], NN)
+        keep = per_level(keep_ref[i], nlev)
+        for f in range(nf):
+            add = proj[f * m : (f + 1) * m] + tend[f] * keep
+            t_ref[f, pl.ds(i * chunk, chunk)] = fv[f, pl.ds(i * chunk, chunk)] + add.reshape(chunk, nlev, lon)
+        return carry
+
+    lax.fori_loop(0, steps, local, 0)
+
     def finish(i, carry):
-        for off in range(n_off):
-            far_copy(off, i).wait()
+        @pl.when(polar(lat_pos, lats, rows, chunk, i))
+        def _():
+            for off in range(n_off):
+                far_copy(off, i).wait()
+
         return carry
 
     lax.fori_loop(0, steps, finish, 0)
 
 
-def second_kernel(ranks, f_ref, t_ref, c_ref, s_ref, keep_ref, wt_ref, thi, tlo, ihi, ilo, v_ref, *rest):
+def second_kernel(ranks, on_ref, t_ref, c_ref, s_ref, v_ref, *rest):
     h_refs, o_ref = rest[:-1], rest[-1]
-    nf, chunk, nlev, lon = f_ref.shape
+    nf, chunk, nlev, lon = t_ref.shape
     m = chunk * nlev
-    tend = [t_ref[f].reshape(m, lon) for f in range(nf)]
-    hi, lo = split(jnp.concatenate(tend, axis=0))
-    spec = dot(hi, thi[...], NN) + dot(hi, tlo[...], NN) + dot(lo, thi[...], NN)
-    wt = per_level(wt_ref[0], nlev)
-    spec = jnp.concatenate([spec[f * m : (f + 1) * m] * wt for f in range(nf)], axis=0)
-    hi, lo = split(spec)
-    local = dot(hi, ihi[...], NN) + dot(hi, ilo[...], NN) + dot(lo, ihi[...], NN)
-    far = []
-    spare = v_ref.shape[0] // 3 - sum(ranks)
-    for part in range(2):
-        h = [ref[0, part * r : (part + 1) * r] for ref, r in zip(h_refs, ranks)]
-        if spare:
-            h.append(jnp.zeros((spare, nf * m), F32))
-        hi, lo = split(jnp.concatenate(h, axis=0))
-        far.append(dot(jnp.concatenate([hi, lo, hi], axis=0), v_ref[...], TN))
-    c, s, keep = (per_level(x[0], nlev) for x in (c_ref, s_ref, keep_ref))
-    for f in range(nf):
-        at = slice(f * m, (f + 1) * m)
-        add = local[at] + far[0][at] * s - far[1][at] * c + tend[f] * keep
-        o_ref[f] = f_ref[f] + add.reshape(chunk, nlev, lon)
+    active = on_ref[pl.program_id(0)] != 0
+
+    @pl.when(active)
+    def _():
+        far = []
+        spare = v_ref.shape[0] // 3 - sum(ranks)
+        for part in range(2):
+            h = [ref[0, part * r : (part + 1) * r] for ref, r in zip(h_refs, ranks)]
+            if spare:
+                h.append(jnp.zeros((spare, nf * m), F32))
+            hi, lo = split(jnp.concatenate(h, axis=0))
+            far.append(dot(jnp.concatenate([hi, lo, hi], axis=0), v_ref[...], TN))
+        c, s = (per_level(x[0], nlev) for x in (c_ref, s_ref))
+        for f in range(nf):
+            at = slice(f * m, (f + 1) * m)
+            o_ref[f] = t_ref[f] + (far[0][at] * s - far[1][at] * c).reshape(chunk, nlev, lon)
+
+    @pl.when(jnp.logical_not(active))
+    def _():
+        o_ref[...] = t_ref[...]
 
 
 def shards(fields, mask, cutoff):
@@ -294,12 +328,7 @@
     v = np.zeros((padr, lon))
     v[:total] = target
     vhi, vlo = split_np(v)
-    flip, at = [], 0
-    for off, r in zip(range(1, lon_count), ranks):
-        flip.append(jnp.where(lon_pos >= off, 1.0, -1.0) * jnp.ones((r,)))
-    flip = jnp.concatenate(flip + [jnp.ones((padr - total,))])
-    flip = jnp.concatenate([flip] * 3).astype(BF16)[:, None]
-    v = jnp.asarray(np.concatenate([vhi, vhi, vlo], axis=0)) * flip
+    v = jnp.asarray(np.concatenate([vhi, vhi, vlo], axis=0))
     angle = (np.arange(lon)[:, None] * np.arange(KMAX)[None, :] % nlon) * (2.0 * math.pi / nlon)
     table = np.concatenate([np.cos(angle), np.sin(angle)], axis=1)
     thi, tlo = split_np(table)
@@ -315,11 +344,12 @@
     m = nf * chunk * nlev
     params = pltpu.CompilerParams(vmem_limit_bytes=32 * 1024 * 1024)
     u = jnp.asarray(u)
+    tables = [jnp.asarray(x) for x in (thi, tlo, ihi, ilo)]
     n_off = len(ranks)
     vmem, far = pl.BlockSpec(memory_space=pltpu.VMEM), pl.BlockSpec(memory_space=pl.ANY)
     out = pl.pallas_call(
         functools.partial(first_kernel, ranks, 1.0 / (2.0 * dlon), 1.0 / (2.0 * dlat), chunk),
-        in_specs=[far] + [vmem] * 4,
+        in_specs=[far] + [vmem] * 10,
         out_specs=[vmem] + [far] * n_off,
         out_shape=[jax.ShapeDtypeStruct(fields.shape, F32)]
         + [jax.ShapeDtypeStruct((steps, 2 * r, m), F32) for r in ranks],
@@ -344,20 +374,19 @@
             vmem_limit_bytes=48 * 1024 * 1024, collective_id=0, has_side_effects=True
         ),
         name="tendency",
-    )(fields, cosine, cphase, sphase, u)
+    )(fields, cosine, cphase, sphase, u, keep, weights, *tables)
     tend, got = out[0], out[1:]
-    shared = [jnp.asarray(x) for x in (thi, tlo, ihi, ilo)] + [v]
+    active = polar(lat_pos, lat_count, rows, chunk, jnp.arange(steps)).astype(jnp.int32)
     out = pl.pallas_call(
         functools.partial(second_kernel, ranks),
         grid=(steps,),
-        in_specs=[band, band, stage(chunk, lon), stage(chunk, lon), stage(chunk, lon), stage(chunk, 2 * KMAX)]
-        + [whole(x) for x in shared]
+        in_specs=[pl.BlockSpec(memory_space=pltpu.SMEM), band, stage(chunk, lon), stage(chunk, lon), whole(v)]
         + [stage(2 * r, m) for r in ranks],
         out_specs=band,
         out_shape=jax.ShapeDtypeStruct(fields.shape, F32),
         compiler_params=params,
         name="projection",
-    )(fields, tend, con, son, keep, weights, *shared, *got)
+    )(active, tend, con, son, v, *got)
     return jnp.transpose(out, (0, 2, 1, 3))
 
 

time: 47.6 us -> 46.5 us (0.977)
  local copies, waits for them, and re-layouts: 4.69 us -> 8.52 us
  Pallas kernels: 39.1 us -> 35.3 us
  other arithmetic: 3.47 us -> 2.23 us
    pallas_call x1, Pallas kernels: 13.6 us -> 5.43 us  [shards(): pl.pallas_call(functools.partial(second_kernel, ranks), grid=(steps,), in...]
    pallas_call x1, Pallas kernels: 25.5 us -> 29.9 us  [shards(): pl.pallas_call(functools.partial(first_kernel, ranks, 1.0 / (2.0 * dlon),...]
    unnamed x14, local copies, waits for them, and re-layouts: 3.59 us -> 7.54 us
    mul x1 -> x0, other arithmetic: 1.18 us -> none  [shards(): v = jnp.asarray(np.concatenate([vhi, vhi, vlo], axis=0)) * flip]
where the time goes in v4:
time: 46.5 us; the launch traced here: 46.1 us
  Pallas kernels  35.3 us (76%)
  local copies, waits for them, and re-layouts  8.52 us (18%)
  other arithmetic  2.23 us (5%)
    pallas_call x1, Pallas kernels, shards(): pl.pallas_call(functools.partial(first_kernel, ranks, 1.0 / (2.0 * dlon),...  29.9 us
    unnamed x14, local copies, waits for them, and re-layouts  7.54 us
    pallas_call x1, Pallas kernels, shards(): pl.pallas_call(functools.partial(second_kernel, ranks), grid=(steps,), in...  5.43 us

profile of v4, /device:TPU:0, one launch (start us, length us, event | category | flops | bytes accessed | tf_op | source)
XLA Modules:
  0.0 46.1 jit_solution(6754193416840402265)
XLA Ops:
  0.0 0.0 copy-start.5
  0.0 0.7 %convert_multiply_fusion = f32[30]{0:T(128)S(1)} fusion(s32[30]{0:T(128)} %param.11), kind=kLoop, calls=%fused_computation.22 | loop fusion | flops 60 | bytes 240 | tf_op jit(solution)/shard_map/mul | solution.py:312
  0.7 0.1 mul.117
  0.8 0.7 %add_cosine_fusion = f32[5,8]{1,0:T(8,128)S(1)} fusion(s32[5,8]{1,0:T(8,128)} %constant.70.clone, s32[]{:T(128)S(6)} %mul.102), kind=kLoop, calls=%fused_computation.17 | loop fusion | flops 240 | bytes 324 | tf_op jit(solution)/shard_map/cos | solution.py:309
  1.5 0.7 %broadcast_in_dim_reshape.4 = s32[5,6]{1,0:T(8,128)S(1)} reshape(s32[30]{0:T(128)} %param.12) | data formatting | bytes 240 | tf_op jit(solution)/shard_map/broadcast_in_dim;reshape | solution.py:314
  2.3 0.1 select_multiply_fusion
  2.4 0.1 broadcast_in_dim.11.keep_ref
  2.4 0.1 broadcast_in_dim.10.cos_ref
  2.6 0.6 %sine_multiply_fusion = (f32[5,6,768]{2,1,0:T(8,128)S(1)}, f32[5,6,768]{2,1,0:T(8,128)S(1)}) fusion(f32[768]{0:T(1024)S(1)} %fusion.5, s32[768]{0:T(1024)S(1)} %iota_add_fusion, s32[5,6]{1,0:T(8,128)S(1)} %multiply_add_fusion), kind=kLoop, calls=%fused_computation.5 | loop fusion | flops 253440 | bytes 190584 | tf_op jit(solution)/shard_map/mul | solution.py:317
  3.2 0.1 slice_multiply_fusion
  3.3 0.0 copy-start.1
  3.3 1.0 %copy-done.1 = bf16[256,720]{1,0:T(8,128)(2,1)S(1)} copy-done((bf16[256,720]{1,0:T(8,128)(2,1)S(1)}, bf16[256,720]{1,0:T(8,128)(2,1)}, u32[]{:S(2)}) %copy-start.1) | copy-done | bytes 368664
  4.3 0.0 copy-start.2
  4.3 1.0 %copy-done.2 = bf16[256,720]{1,0:T(8,128)(2,1)S(1)} copy-done((bf16[256,720]{1,0:T(8,128)(2,1)S(1)}, bf16[256,720]{1,0:T(8,128)(2,1)}, u32[]{:S(2)}) %copy-start.2) | copy-done | bytes 368664
  5.2 0.0 copy-start.3
  5.2 1.0 %copy-done.3 = bf16[720,256]{1,0:T(8,128)(2,1)S(1)} copy-done((bf16[720,256]{1,0:T(8,128)(2,1)S(1)}, bf16[720,256]{1,0:T(8,128)(2,1)}, u32[]{:S(2)}) %copy-start.3) | copy-done | bytes 368664
  6.2 0.0 copy-start.4
  6.2 1.0 %copy-done.4 = bf16[720,256]{1,0:T(8,128)(2,1)S(1)} copy-done((bf16[720,256]{1,0:T(8,128)(2,1)S(1)}, bf16[720,256]{1,0:T(8,128)(2,1)}, u32[]{:S(2)}) %copy-start.4) | copy-done | bytes 368664
  7.2 0.9 %copy-done.6 = bf16[96,768]{1,0:T(8,128)(2,1)S(1)} copy-done((bf16[96,768]{1,0:T(8,128)(2,1)S(1)}, bf16[96,768]{1,0:T(8,128)(2,1)}, u32[]{:S(2)}) %copy-start.6) | copy-done | bytes 147480
  8.1 29.9 %tendency.1 = (f32[8,30,8,720]{3,2,1,0:T(8,128)}, f32[5,32,384]{2,1,0:T(8,128)S(1)}, f32[5,16,384]{2,1,0:T(8,128)S(1)}, f32[5,32,384]{2,1,0:T(8,128)S(1)}) custom-call(f32[8,30,8,720]{3,2,1,0:T(8,128)} %bitcast.2, f32[5,8,8,128]{3,2,1,0:T(8,128)S(1)} %broadcast_in_dim.10.cos_ref, f32[5,6,768]{2,1,0:T(8,128)S(1)} %get-tuple-element.14.c_ref, ...), custom_call_target="tpu_custom_call" | custom-call | tf_op jit(solution)/shard_map/tendency/pallas_call | solution.py:350
  38.0 0.0 copy-done.5
  38.0 0.0 copy-start
  38.0 2.7 %copy-done = f32[8,30,8,720]{3,2,1,0:T(8,128)S(1)} copy-done((f32[8,30,8,720]{3,2,1,0:T(8,128)S(1)}, f32[8,30,8,720]{3,2,1,0:T(8,128)}, u32[]{:S(2)}) %copy-start) | copy-done | bytes 5529624
  40.7 5.4 %projection.1 = f32[8,30,8,720]{3,2,1,0:T(8,128)} custom-call(s32[5]{0:T(128)S(1)} %or_convert_fusion.on_ref, f32[8,30,8,720]{3,2,1,0:T(8,128)S(1)} %copy-done, f32[5,6,720]{2,1,0:T(8,128)S(1)} %get-tuple-element.16.c_ref, f32[5,6,720]{2,1,0:T(8,128)S(1)} %get-tuple-element.15.s_ref, bf16[144,720]{1,0:T(8,128)(2,1)S(1)} %copy-done.5, ...), custom_call_target="tpu_custom_call" | custom-call | tf_op jit(solution)/shard_map/projection/pallas_call | solution.py:380
  (8 shorter events, 0.0 us)
Async XLA Ops:
  0.0 38.0 %copy-start.5 = (bf16[144,720]{1,0:T(8,128)(2,1)S(1)}, bf16[144,720]{1,0:T(8,128)(2,1)}, u32[]{:S(2)}) copy-start(bf16[144,720]{1,0:T(8,128)(2,1)} %constant.71.clone.v_ref) | copy-start | bytes 622084
  3.3 1.0 %copy-start.1 = (bf16[256,720]{1,0:T(8,128)(2,1)S(1)}, bf16[256,720]{1,0:T(8,128)(2,1)}, u32[]{:S(2)}) copy-start(bf16[256,720]{1,0:T(8,128)(2,1)} %constant.76.clone.ilo) | copy-start | bytes 1105924
  4.3 1.0 %copy-start.2 = (bf16[256,720]{1,0:T(8,128)(2,1)S(1)}, bf16[256,720]{1,0:T(8,128)(2,1)}, u32[]{:S(2)}) copy-start(bf16[256,720]{1,0:T(8,128)(2,1)} %constant.75.clone.ihi) | copy-start | bytes 1105924
  5.2 1.0 %copy-start.3 = (bf16[720,256]{1,0:T(8,128)(2,1)S(1)}, bf16[720,256]{1,0:T(8,128)(2,1)}, u32[]{:S(2)}) copy-start(bf16[720,256]{1,0:T(8,128)(2,1)} %constant.74.clone.tlo) | copy-start | bytes 1105924
  6.2 1.0 %copy-start.4 = (bf16[720,256]{1,0:T(8,128)(2,1)S(1)}, bf16[720,256]{1,0:T(8,128)(2,1)}, u32[]{:S(2)}) copy-start(bf16[720,256]{1,0:T(8,128)(2,1)} %constant.73.clone.thi) | copy-start | bytes 1105924
  7.2 0.9 %copy-start.6 = (bf16[96,768]{1,0:T(8,128)(2,1)S(1)}, bf16[96,768]{1,0:T(8,128)(2,1)}, u32[]{:S(2)}) copy-start(bf16[96,768]{1,0:T(8,128)(2,1)} %constant.72.clone.u_ref) | copy-start | bytes 442372
  38.0 2.7 %copy-start = (f32[8,30,8,720]{3,2,1,0:T(8,128)S(1)}, f32[8,30,8,720]{3,2,1,0:T(8,128)}, u32[]{:S(2)}) copy-start(f32[8,30,8,720]{3,2,1,0:T(8,128)} %get-tuple-element.9.t_ref) | copy-start | bytes 16588804

commit v5 on v4

--- a/solution.py
+++ b/solution.py
@@ -69,8 +69,12 @@
 
 
 def first_kernel(
-    ranks, a, b, chunk, f_any, cos_ref, c_ref, s_ref, u_ref, keep_ref, wt_ref, thi, tlo, ihi, ilo, t_ref, *rest
+    ranks, a, b, chunk, f_any, cos_ref, c_ref, s_ref, keep_ref, wt_ref, *rest
 ):
+    tables_any, t_any, rest = rest[:5], rest[5], rest[6:]
+    u_ref, thi, tlo, ihi, ilo = tables = rest[-8:-3]
+    table_sem, t_ref, out_sem = rest[-3:]
+    rest = rest[:-8]
     n_off = len(ranks)
     got, (fv, w, halo, edge, ghost), held = rest[:n_off], rest[n_off : n_off + 5], rest[n_off + 5 : 2 * n_off + 5]
     load_sem, row_send, row_recv, col_send, col_recv, far_send, far_recv = rest[2 * n_off + 5 :]
@@ -87,6 +91,9 @@
 
     load = pltpu.make_async_copy(f_any, fv, load_sem)
     load.start()
+    moves = [pltpu.make_async_copy(x, y, table_sem.at[n]) for n, (x, y) in enumerate(zip(tables_any, tables))]
+    for move in moves:
+        move.start()
     barrier = pltpu.get_barrier_semaphore()
 
     def greet(lat, lon_at):
@@ -166,6 +173,8 @@
         row_copy(0, which, lat_pos, opposite, which).wait()
     for copy in cols:
         copy.wait()
+    for move in moves:
+        move.wait()
     turn_low = jnp.where(lat_pos == 0, -1.0, 1.0)
     turn_high = jnp.where(lat_pos == lats - 1, -1.0, 1.0)
 
@@ -234,6 +243,10 @@
 
     lax.fori_loop(0, steps, work, 0)
 
+    def out_copy(i):
+        at = pl.ds(i * chunk, chunk)
+        return pltpu.make_async_copy(t_ref.at[:, at], t_any.at[:, at], out_sem.at[i])
+
     def local(i, carry):
         m = chunk * nlev
         tend = [t_ref[f, pl.ds(i * chunk, chunk)].reshape(m, lon) for f in range(nf)]
@@ -247,11 +260,14 @@
         for f in range(nf):
             add = proj[f * m : (f + 1) * m] + tend[f] * keep
             t_ref[f, pl.ds(i * chunk, chunk)] = fv[f, pl.ds(i * chunk, chunk)] + add.reshape(chunk, nlev, lon)
+        out_copy(i).start()
         return carry
 
     lax.fori_loop(0, steps, local, 0)
 
     def finish(i, carry):
+        out_copy(i).wait()
+
         @pl.when(polar(lat_pos, lats, rows, chunk, i))
         def _():
             for off in range(n_off):
@@ -342,15 +358,15 @@
 
     band = pl.BlockSpec((nf, chunk, nlev, lon), lambda i: (0, i, 0, 0))
     m = nf * chunk * nlev
-    params = pltpu.CompilerParams(vmem_limit_bytes=32 * 1024 * 1024)
+    params = pltpu.CompilerParams(vmem_limit_bytes=60 * 1024 * 1024)
     u = jnp.asarray(u)
-    tables = [jnp.asarray(x) for x in (thi, tlo, ihi, ilo)]
+    tables = [u] + [jnp.asarray(x) for x in (thi, tlo, ihi, ilo)]
     n_off = len(ranks)
     vmem, far = pl.BlockSpec(memory_space=pltpu.VMEM), pl.BlockSpec(memory_space=pl.ANY)
     out = pl.pallas_call(
         functools.partial(first_kernel, ranks, 1.0 / (2.0 * dlon), 1.0 / (2.0 * dlat), chunk),
-        in_specs=[far] + [vmem] * 10,
-        out_specs=[vmem] + [far] * n_off,
+        in_specs=[far] + [vmem] * 5 + [far] * 5,
+        out_specs=[far] * (n_off + 1),
         out_shape=[jax.ShapeDtypeStruct(fields.shape, F32)]
         + [jax.ShapeDtypeStruct((steps, 2 * r, m), F32) for r in ranks],
         scratch_shapes=[
@@ -369,12 +385,14 @@
             pltpu.SemaphoreType.DMA((2,)),
             pltpu.SemaphoreType.DMA((n_off, steps)),
             pltpu.SemaphoreType.DMA((n_off, steps)),
-        ],
+        ]
+        + [pltpu.VMEM(x.shape, BF16) for x in tables]
+        + [pltpu.SemaphoreType.DMA((5,)), pltpu.VMEM(fields.shape, F32), pltpu.SemaphoreType.DMA((steps,))],
         compiler_params=pltpu.CompilerParams(
-            vmem_limit_bytes=48 * 1024 * 1024, collective_id=0, has_side_effects=True
+            vmem_limit_bytes=60 * 1024 * 1024, collective_id=0, has_side_effects=True
         ),
         name="tendency",
-    )(fields, cosine, cphase, sphase, u, keep, weights, *tables)
+    )(fields, cosine, cphase, sphase, keep, weights, *tables)
     tend, got = out[0], out[1:]
     active = polar(lat_pos, lat_count, rows, chunk, jnp.arange(steps)).astype(jnp.int32)
     out = pl.pallas_call(

time: 46.5 us -> 45 us (0.968)
  local copies, waits for them, and re-layouts: 8.52 us -> 2.31 us
  Pallas kernels: 35.3 us -> 38.4 us
  other arithmetic: 2.23 us -> 4.01 us
    unnamed x14 -> x4, local copies, waits for them, and re-layouts: 7.54 us -> 0.01 us
    pallas_call x1, Pallas kernels: 5.43 us -> 8.38 us  [shards(): pl.pallas_call(functools.partial(second_kernel, ranks), grid=(steps,), in...]
    mul x1, other arithmetic: 0.09 us -> 0.78 us  [shards(): sphase[:, :, :lon] * on[:, :, None]]
    broadcast_in_dim x1, local copies, waits for them, and re-layouts: 0.1 us -> 0.77 us  [shards(): jnp.broadcast_to(cosine[:, :, None, None], (steps, chunk + 2, nlev, 128))]
    broadcast_in_dim x1, local copies, waits for them, and re-layouts: 0.07 us -> 0.72 us  [shards(): keep = jnp.broadcast_to((step - on)[:, :, None], (steps, chunk, lon))]
    concatenate x1, other arithmetic: 0.01 us -> 0.63 us  [shards(): weights = jnp.concatenate([weights, weights], axis=2)]
    convert_element_type x1, other arithmetic: 0.01 us -> 0.52 us  [shards(): polar(lat_pos, lat_count, rows, chunk, jnp.arange(steps)).astype(jnp.int32)]
where the time goes in v5:
time: 45 us; the launch traced here: 44.7 us
  Pallas kernels  38.4 us (85%)
  other arithmetic  4.01 us (9%)
  local copies, waits for them, and re-layouts  2.31 us (5%)
    pallas_call x1, Pallas kernels, shards(): pl.pallas_call(functools.partial(first_kernel, ranks, 1.0 / (2.0 * dlon),...  30 us
    pallas_call x1, Pallas kernels, shards(): pl.pallas_call(functools.partial(second_kernel, ranks), grid=(steps,), in...  8.38 us

profile of v5, /device:TPU:0, one launch (start us, length us, event | category | flops | bytes accessed | tf_op | source)
XLA Modules:
  0.0 44.7 jit_solution(3167729632799197088)
XLA Ops:
  0.0 0.7 %convert_multiply_fusion = f32[30]{0:T(128)S(1)} fusion(s32[30]{0:T(128)} %param.11), kind=kLoop, calls=%fused_computation.22 | loop fusion | flops 60 | bytes 240 | tf_op jit(solution)/shard_map/mul | solution.py:328
  0.7 0.5 %or_convert_fusion.on_ref = s32[5]{0:T(128)} fusion(s32[]{:T(128)S(6)} %mul.102), kind=kLoop, calls=%fused_computation.21 | loop fusion | flops 35 | bytes 24 | tf_op jit(solution)/shard_map/convert_element_type | solution.py:397
  1.2 0.1 mul.117
  1.3 0.7 %add_cosine_fusion = f32[5,8]{1,0:T(8,128)S(1)} fusion(s32[5,8]{1,0:T(8,128)} %constant.70.clone, s32[]{:T(128)S(6)} %mul.102), kind=kLoop, calls=%fused_computation.17 | loop fusion | flops 240 | bytes 324 | tf_op jit(solution)/shard_map/cos | solution.py:325
  2.0 0.7 %broadcast_in_dim_reshape.4 = s32[5,6]{1,0:T(8,128)S(1)} reshape(s32[30]{0:T(128)} %param.12) | data formatting | bytes 240 | tf_op jit(solution)/shard_map/broadcast_in_dim;reshape | solution.py:330
  2.8 0.1 select_multiply_fusion
  2.8 0.6 %pad_maximum_fusion.wt_ref = f32[5,6,256]{2,1,0:T(8,128)} fusion(f32[5,6,128]{2,1,0:T(8,128)S(1)} %select_multiply_fusion), kind=kLoop, calls=%fused_computation.11 | loop fusion | flops 7680 | bytes 46080 | tf_op jit(solution)/shard_map/concatenate | solution.py:339
  3.5 0.7 %broadcast_in_dim.11.keep_ref = f32[5,6,720]{2,1,0:T(8,128)} broadcast(f32[5,6]{1,0:T(8,128)S(1)} %broadcast_subtract_fusion), dimensions={0,1} | broadcast | bytes 86520 | tf_op jit(solution)/shard_map/broadcast_in_dim | solution.py:335
  4.2 0.8 %broadcast_in_dim.10.cos_ref = f32[5,8,8,128]{3,2,1,0:T(8,128)} broadcast(f32[5,8]{1,0:T(8,128)S(1)} %add_cosine_fusion), dimensions={0,1} | broadcast | bytes 164000 | tf_op jit(solution)/shard_map/broadcast_in_dim | solution.py:326
  5.0 0.6 %sine_multiply_fusion = (f32[5,6,768]{2,1,0:T(8,128)S(1)}, f32[5,6,768]{2,1,0:T(8,128)S(1)}) fusion(f32[768]{0:T(1024)S(1)} %fusion.5, s32[768]{0:T(1024)S(1)} %iota_add_fusion, s32[5,6]{1,0:T(8,128)S(1)} %multiply_add_fusion), kind=kLoop, calls=%fused_computation.5 | loop fusion | flops 253440 | bytes 190584 | tf_op jit(solution)/shard_map/mul | solution.py:333
  5.6 0.0 copy-start
  5.6 0.0 copy-start.1
  5.6 0.8 %slice_multiply_fusion = (f32[5,6,720]{2,1,0:T(8,128)}, f32[5,6,720]{2,1,0:T(8,128)}) fusion(f32[5,6,768]{2,1,0:T(8,128)S(1)} %get-tuple-element.13.s_ref, f32[5,6]{1,0:T(8,128)S(1)} %mul.117, f32[5,6,768]{2,1,0:T(8,128)S(1)} %get-tuple-element.14.c_ref), kind=kLoop, calls=%fused_computation.3 | loop fusion | flops 43200 | bytes 345720 | tf_op jit(solution)/shard_map/mul | solution.py:334
  6.4 0.0 copy-done
  6.4 0.0 copy-done.1
  6.4 30.0 %tendency.1 = (f32[8,30,8,720]{3,2,1,0:T(8,128)}, f32[5,32,384]{2,1,0:T(8,128)}, f32[5,16,384]{2,1,0:T(8,128)}, f32[5,32,384]{2,1,0:T(8,128)}) custom-call(f32[8,30,8,720]{3,2,1,0:T(8,128)} %bitcast.2, f32[5,8,8,128]{3,2,1,0:T(8,128)} %broadcast_in_dim.10.cos_ref, f32[5,6,768]{2,1,0:T(8,128)} %copy-done.1, f32[5,6,768]{2,1,0:T(8,128)} %copy-done, ...), custom_call_target="tpu_custom_call" | custom-call | tf_op jit(solution)/shard_map/tendency/pallas_call | solution.py:366
  36.4 8.4 %projection.1 = f32[8,30,8,720]{3,2,1,0:T(8,128)} custom-call(s32[5]{0:T(128)} %or_convert_fusion.on_ref, f32[8,30,8,720]{3,2,1,0:T(8,128)} %get-tuple-element.9.t_ref, f32[5,6,720]{2,1,0:T(8,128)} %get-tuple-element.16.c_ref, f32[5,6,720]{2,1,0:T(8,128)} %get-tuple-element.15.s_ref, bf16[144,720]{1,0:T(8,128)(2,1)} %constant.71.clone.v_ref, ...), custom_call_target="tpu_custom_call" | custom-call | tf_op jit(solution)/shard_map/projection/pallas_call | solution.py:398
  (5 shorter events, 0.0 us)
Async XLA Ops:
  5.6 0.8 %copy-start = (f32[5,6,768]{2,1,0:T(8,128)}, f32[5,6,768]{2,1,0:T(8,128)S(1)}, u32[]{:S(2)}) copy-start(f32[5,6,768]{2,1,0:T(8,128)S(1)} %get-tuple-element.13.s_ref) | copy-start | bytes 276484
  5.6 0.8 %copy-start.1 = (f32[5,6,768]{2,1,0:T(8,128)}, f32[5,6,768]{2,1,0:T(8,128)S(1)}, u32[]{:S(2)}) copy-start(f32[5,6,768]{2,1,0:T(8,128)S(1)} %get-tuple-element.14.c_ref) | copy-start | bytes 276484
